TPU v7x, 128 devices: a whole 4x4x4 slice. The times are simulated.
128 devices in a mesh: section: 2 (over z_lo), expert: 16 (over x, y), shard: 4 (over z_hi, core).
Axes of the slice: x: 4, y: 4, z: 4 (z_hi: 2, z_lo: 2; z = z_hi * 2 + z_lo), core: 2. Of those that a mesh axis runs over, the one named last changes fastest.
Arguments:
- images: bfloat16 [2, 256, 50, 512], P(None, ('expert', 'shard')), may hold values from -6 to 6
- cotangent: bfloat16 [2, 256, 50, 512], P(None, ('expert', 'shard')), may hold values from -6 to 6
- ln1_gain: bfloat16 [2, 512], P('section', 'shard'), may hold values from 0.5 to 1.5
- qkv_weight: bfloat16 [2, 512, 1536], P('section', 'shard'), may hold values from -0.25 to 0.25
- out_weight: bfloat16 [2, 512, 512], P('section', 'shard'), may hold values from -0.75 to 0.75
- ln2_gain: bfloat16 [2, 512], P('section', 'shard'), may hold values from 0.5 to 1.5
- router_weight: bfloat16 [2, 512, 32], P('section', 'shard'), may hold values from -0.1875 to 0.1875
- up_weight: bfloat16 [2, 32, 2048, 512], P('section', 'expert', 'shard'), may hold values from -0.25 to 0.25
- down_weight: bfloat16 [2, 32, 2048, 512], P('section', 'expert', 'shard'), may hold values from -0.25 to 0.25
- routes: int32 [2, 2, 256, 50, 2], P('section', None, ('expert', 'shard')), may hold values from 0 to 31, all different within a row; in each aligned block of 200 rows (0 to 199, 200 to 399, ..., all dimensions but the last counted through in order) at most 14 rows name the same one
Outputs:
- layer_out: bfloat16 [2, 2, 256, 50, 512], P('section', None, ('expert', 'shard'))
- layer_in_grad: bfloat16 [2, 2, 256, 50, 512], P('section', None, ('expert', 'shard'))
- ln1_gain_grad: float32 [2, 512], P('section', 'shard')
- qkv_weight_grad: float32 [2, 512, 1536], P('section', 'shard')
- out_weight_grad: float32 [2, 512, 512], P('section', 'shard')
- ln2_gain_grad: float32 [2, 512], P('section', 'shard')
- router_weight_grad: float32 [2, 512, 32], P('section', 'shard')
- up_weight_grad: float32 [2, 32, 2048, 512], P('section', 'expert', 'shard')
- down_weight_grad: float32 [2, 32, 2048, 512], P('section', 'expert', 'shard')
Inputs may be any that keep to these rules, and one draw needn't show every extreme that they name: `routes`: in each aligned block of 200 tokens (the tokens of one device in one micro-batch of one layer) no expert is named by more than 14 tokens, a bound that some block reaches; the 2 experts of a token differ.
All inputs are finite; a program needn't handle non-finite values.
Results may differ from a plain program's by a relative error of at most 0.03.
Values may be sent and summed in bfloat16 or wider, within the bound.
A program may use at most 128 MiB of HBM per device.

v0:
```python
import jax
import jax.numpy as jnp
from jax import lax
from jax.sharding import PartitionSpec as P

HEADS = 8
HEAD_DIM = 64
TOPK = 2
SEQ = 50


epsilon = 1e-06


def from_behind(value, axis, steps):
    count = lax.axis_size(axis)
    initial, last = (max(0, -steps), min(count, count - steps))
    return lax.ppermute(value, axis, [(source, source + steps) for source in range(initial, last)])


def normalize(values):
    center = jnp.mean(values, axis=-1, keepdims=True)
    shifted = values - center
    inverse = lax.rsqrt(jnp.mean(shifted * shifted, axis=-1, keepdims=True) + epsilon)
    return (shifted * inverse, inverse)


def norm_back(grad_normed, normed, inverse):
    mean_grad = jnp.mean(grad_normed, axis=-1, keepdims=True)
    mean_cross = jnp.mean(grad_normed * normed, axis=-1, keepdims=True)
    return inverse * (grad_normed - mean_grad - normed * mean_cross)


def expert_apply(inputs, up_part, down_part):
    before = jnp.einsum("secd,efd->secf", inputs, up_part, preferred_element_type=jnp.float32)
    active = jax.nn.gelu(before).astype(jnp.bfloat16)
    return jnp.einsum("secf,efd->secd", active, down_part, preferred_element_type=jnp.float32)


def expert_grads(inputs, grad_output, up_part, down_part):
    before = jnp.einsum("secd,efd->secf", inputs, up_part, preferred_element_type=jnp.float32)
    active, gelu_pull = jax.vjp(jax.nn.gelu, before)
    grad_down = jnp.einsum(
        "secf,secd->efd",
        active.astype(jnp.bfloat16),
        grad_output,
        preferred_element_type=jnp.float32,
    )
    grad_active = jnp.einsum(
        "secd,efd->secf", grad_output, down_part, preferred_element_type=jnp.float32
    )
    grad_before = gelu_pull(grad_active)[0].astype(jnp.bfloat16)
    grad_up = jnp.einsum("secf,secd->efd", grad_before, inputs, preferred_element_type=jnp.float32)
    return (grad_before, grad_up, grad_down)


def to_experts(values):
    return lax.all_to_all(values, "expert", split_axis=0, concat_axis=0, tiled=True)


def from_experts(values):
    return lax.all_to_all(values, "expert", split_axis=0, concat_axis=0, tiled=True)


def expert_forward(received, up_local, down_local):

    def add_piece(running, pieces, first_col):
        return expert_apply(received, pieces[0], pieces[1])

    initial = jnp.zeros(received.shape, jnp.float32)
    summed = add_piece(
        initial,
        (
            lax.all_gather(up_local, "shard", axis=1, tiled=True),
            lax.all_gather(down_local, "shard", axis=1, tiled=True),
        ),
        jnp.int32(0),
    )
    return (summed.astype(jnp.bfloat16), received)


def expert_backward(kept_rows, grad_received, up_local, down_local, grad_up, grad_down):

    def add_piece(carried, pieces, first_col):
        grad_rows, full_up, full_down = carried
        grad_before, piece_up, piece_down = expert_grads(
            kept_rows, grad_received, pieces[0], pieces[1]
        )
        span_cols = pieces[0].shape[1]
        full_up = full_up + piece_up
        full_down = full_down + piece_down
        grad_rows = jnp.einsum(
            "secf,efd->secd", grad_before, pieces[0], preferred_element_type=jnp.float32
        )
        return (grad_rows, full_up, full_down)

    initial = (jnp.zeros(grad_received.shape, jnp.float32), grad_up, grad_down)
    grad_rows, grad_up, grad_down = add_piece(
        initial,
        (
            lax.all_gather(up_local, "shard", axis=1, tiled=True),
            lax.all_gather(down_local, "shard", axis=1, tiled=True),
        ),
        jnp.int32(0),
    )
    return (grad_rows.astype(jnp.bfloat16), grad_up, grad_down)


def placement_matrix(route_rows, experts, capacity):
    flat_routes = route_rows.reshape(-1)
    choose = (flat_routes[:, None] == jnp.arange(experts, dtype=jnp.int32)[None, :]).astype(
        jnp.int32
    )
    earlier = jnp.cumsum(choose, axis=0) - choose
    slot_index = jnp.sum(earlier * choose, axis=1)
    target = flat_routes * capacity + slot_index
    return (jnp.arange(experts * capacity, dtype=jnp.int32)[:, None] == target[None, :]).astype(
        jnp.bfloat16
    )


def layer_forward(rows_in, route_rows, shared, up_local, down_local):
    gain_one, weight_qkv, weight_out, gain_two, weight_router = shared
    row_count, model_width = rows_in.shape
    images_here = row_count // SEQ
    experts = weight_router.shape[1]
    capacity = row_count * TOPK // experts + 2
    scaling = HEAD_DIM ** (-0.5)
    normed_one, inverse_one = normalize(rows_in)
    first_in = (normed_one * gain_one.astype(jnp.float32)).astype(jnp.bfloat16)
    mixed_qkv = jnp.dot(first_in, weight_qkv, preferred_element_type=jnp.float32).astype(
        jnp.bfloat16
    )
    mixed_qkv = mixed_qkv.reshape(images_here, SEQ, 3, HEADS, HEAD_DIM)
    scores = (
        jnp.einsum(
            "bqhd,bkhd->bhqk",
            mixed_qkv[:, :, 0],
            mixed_qkv[:, :, 1],
            preferred_element_type=jnp.float32,
        )
        * scaling
    )
    highest = jnp.max(scores, axis=-1, keepdims=True)
    raised = jnp.exp(scores - highest)
    totals = jnp.sum(raised, axis=-1, keepdims=True)
    probability = raised / totals
    log_total = highest + jnp.log(totals)
    attended = jnp.einsum(
        "bhqk,bkhd->bqhd",
        probability.astype(jnp.bfloat16),
        mixed_qkv[:, :, 2],
        preferred_element_type=jnp.float32,
    )
    attended = attended.astype(jnp.bfloat16).reshape(row_count, model_width)
    hidden = rows_in + jnp.dot(attended, weight_out, preferred_element_type=jnp.float32)
    normed_two, inverse_two = normalize(hidden)
    second_in = (normed_two * gain_two.astype(jnp.float32)).astype(jnp.bfloat16)
    logits = jnp.dot(second_in, weight_router, preferred_element_type=jnp.float32)
    choose = (route_rows[:, :, None] == jnp.arange(experts, dtype=jnp.int32)[None, None, :]).astype(
        jnp.float32
    )
    gate_values = jax.nn.softmax(jnp.sum(choose * logits[:, None, :], axis=-1), axis=-1)
    placing = placement_matrix(route_rows, experts, capacity)
    copies = jnp.broadcast_to(second_in[:, None, :], (row_count, TOPK, model_width)).reshape(
        row_count * TOPK, model_width
    )
    buffer = jnp.dot(placing, copies, preferred_element_type=jnp.float32).astype(jnp.bfloat16)
    groups = lax.axis_size("expert")
    received = to_experts(buffer.reshape(groups, experts // groups, capacity, model_width))
    expert_out, kept_rows = expert_forward(received, up_local, down_local)
    returned = from_experts(expert_out).reshape(experts * capacity, model_width)
    picked = jnp.einsum("sn,sd->nd", placing, returned, preferred_element_type=jnp.float32).reshape(
        row_count, TOPK, model_width
    )
    result = hidden + jnp.sum(gate_values[:, :, None] * picked, axis=1)
    kept = (
        normed_one,
        inverse_one,
        first_in,
        mixed_qkv,
        log_total,
        attended,
        normed_two,
        inverse_two,
        second_in,
        choose,
        gate_values,
        placing,
        picked,
        kept_rows,
    )
    return (result, kept)


def layer_backward(grad_out, kept, shared, up_local, down_local, sums):
    (
        normed_one,
        inverse_one,
        first_in,
        mixed_qkv,
        log_total,
        attended,
        normed_two,
        inverse_two,
        second_in,
        choose,
        gate_values,
        placing,
        picked,
        kept_rows,
    ) = kept
    gain_one, weight_qkv, weight_out, gain_two, weight_router = shared
    acc_gain_one, acc_qkv, acc_out, acc_gain_two, acc_router, acc_up, acc_down = sums
    row_count, model_width = grad_out.shape
    images_here = row_count // SEQ
    experts = weight_router.shape[1]
    capacity = placing.shape[0] // experts
    scaling = HEAD_DIM ** (-0.5)
    grad_gate = jnp.sum(grad_out[:, None, :] * picked, axis=-1)
    grad_copies = (
        (gate_values[:, :, None] * grad_out[:, None, :])
        .astype(jnp.bfloat16)
        .reshape(row_count * TOPK, model_width)
    )
    grad_buffer = jnp.dot(placing, grad_copies, preferred_element_type=jnp.float32).astype(
        jnp.bfloat16
    )
    groups = lax.axis_size("expert")
    grad_received = to_experts(
        grad_buffer.reshape(groups, experts // groups, capacity, model_width)
    )
    grad_rows, acc_up, acc_down = expert_backward(
        kept_rows, grad_received, up_local, down_local, acc_up, acc_down
    )
    grad_returned = from_experts(grad_rows).reshape(experts * capacity, model_width)
    grad_sent = jnp.einsum("sn,sd->nd", placing, grad_returned, preferred_element_type=jnp.float32)
    grad_sent = jnp.sum(grad_sent.reshape(row_count, TOPK, model_width), axis=1)
    grad_chosen = gate_values * (
        grad_gate - jnp.sum(gate_values * grad_gate, axis=-1, keepdims=True)
    )
    grad_logits = jnp.sum(choose * grad_chosen[:, :, None], axis=1).astype(jnp.bfloat16)
    acc_router = acc_router + jnp.einsum(
        "nd,ne->de", second_in, grad_logits, preferred_element_type=jnp.float32
    )
    grad_second = grad_sent + jnp.einsum(
        "ne,de->nd", grad_logits, weight_router, preferred_element_type=jnp.float32
    )
    acc_gain_two = acc_gain_two + jnp.sum(grad_second * normed_two, axis=0)
    grad_hidden = grad_out + norm_back(
        grad_second * gain_two.astype(jnp.float32), normed_two, inverse_two
    )
    grad_mixed = grad_hidden.astype(jnp.bfloat16)
    acc_out = acc_out + jnp.einsum(
        "nd,ne->de", attended, grad_mixed, preferred_element_type=jnp.float32
    )
    grad_attended = jnp.einsum(
        "ne,de->nd", grad_mixed, weight_out, preferred_element_type=jnp.float32
    )
    grad_attended = grad_attended.astype(jnp.bfloat16).reshape(images_here, SEQ, HEADS, HEAD_DIM)
    query_heads = mixed_qkv[:, :, 0]
    key_heads = mixed_qkv[:, :, 1]
    value_heads = mixed_qkv[:, :, 2]
    scores = (
        jnp.einsum("bqhd,bkhd->bhqk", query_heads, key_heads, preferred_element_type=jnp.float32)
        * scaling
    )
    probability = jnp.exp(scores - log_total)
    grad_value = jnp.einsum(
        "bhqk,bqhd->bkhd",
        probability.astype(jnp.bfloat16),
        grad_attended,
        preferred_element_type=jnp.float32,
    )
    grad_prob = jnp.einsum(
        "bqhd,bkhd->bhqk", grad_attended, value_heads, preferred_element_type=jnp.float32
    )
    grad_scores = (
        probability * (grad_prob - jnp.sum(probability * grad_prob, axis=-1, keepdims=True))
    ).astype(jnp.bfloat16)
    grad_query = (
        jnp.einsum("bhqk,bkhd->bqhd", grad_scores, key_heads, preferred_element_type=jnp.float32)
        * scaling
    )
    grad_key = (
        jnp.einsum("bhqk,bqhd->bkhd", grad_scores, query_heads, preferred_element_type=jnp.float32)
        * scaling
    )
    grad_qkv = (
        jnp.stack([grad_query, grad_key, grad_value], axis=2)
        .astype(jnp.bfloat16)
        .reshape(row_count, 3 * model_width)
    )
    acc_qkv = acc_qkv + jnp.einsum(
        "nd,ne->de", first_in, grad_qkv, preferred_element_type=jnp.float32
    )
    grad_first = jnp.einsum("ne,de->nd", grad_qkv, weight_qkv, preferred_element_type=jnp.float32)
    acc_gain_one = acc_gain_one + jnp.sum(grad_first * normed_one, axis=0)
    grad_in = grad_hidden + norm_back(
        grad_first * gain_one.astype(jnp.float32), normed_one, inverse_one
    )
    return (grad_in, (acc_gain_one, acc_qkv, acc_out, acc_gain_two, acc_router, acc_up, acc_down))


def shards(
    images,
    cotangent,
    ln1_gain,
    qkv_weight,
    out_weight,
    ln2_gain,
    router_weight,
    up_weight,
    down_weight,
    routes,
):
    shared = (
        lax.all_gather(ln1_gain[0], "shard", axis=0, tiled=True),
        lax.all_gather(qkv_weight[0], "shard", axis=0, tiled=True),
        lax.all_gather(out_weight[0], "shard", axis=0, tiled=True),
        lax.all_gather(ln2_gain[0], "shard", axis=0, tiled=True),
        lax.all_gather(router_weight[0], "shard", axis=0, tiled=True),
    )
    up_local = up_weight[0]
    down_local = down_weight[0]
    layer_routes = routes[0]
    micro_total = images.shape[0]
    row_count = images.shape[1] * images.shape[2]
    model_width = images.shape[3]
    is_first = lax.axis_index("section") == 0
    full_span = up_local.shape[1] * lax.axis_size("shard")
    sums = tuple((jnp.zeros(item.shape, jnp.float32) for item in shared))
    sums = sums + (
        jnp.zeros((up_local.shape[0], full_span, model_width), jnp.float32),
        jnp.zeros((up_local.shape[0], full_span, model_width), jnp.float32),
    )
    incoming = jnp.zeros((row_count, model_width), jnp.bfloat16)
    outputs = []
    kept_all = []
    for tick_no in range(micro_total + 1):
        own_index = min(tick_no, micro_total - 1)
        own_rows = images[own_index].reshape(row_count, model_width)
        rows_in = jnp.where(is_first, own_rows, incoming).astype(jnp.float32)
        micro_index = jnp.where(is_first, own_index, max(tick_no - 1, 0)).astype(jnp.int32)
        route_rows = lax.dynamic_index_in_dim(layer_routes, micro_index, 0, keepdims=False).reshape(
            row_count, TOPK
        )
        result, kept = layer_forward(rows_in, route_rows, shared, up_local, down_local)
        outputs.append(result.astype(jnp.bfloat16))
        kept_all.append(kept)
        if tick_no < micro_total:
            incoming = from_behind(outputs[-1], "section", 1)
    outgoing = jnp.zeros((row_count, model_width), jnp.bfloat16)
    grads_in = []
    for tick_no in range(micro_total + 1):
        if tick_no < micro_total:
            from_loss = cotangent[tick_no].reshape(row_count, model_width)
        else:
            from_loss = jnp.zeros((row_count, model_width), jnp.bfloat16)
        grad_out = jnp.where(is_first, outgoing, from_loss).astype(jnp.float32)
        kept = jax.tree.map(
            lambda early, later: jnp.where(is_first, early, later),
            kept_all[max(tick_no - 1, 0)],
            kept_all[min(tick_no + 1, micro_total)],
        )
        grad_in, sums = layer_backward(grad_out, kept, shared, up_local, down_local, sums)
        grads_in.append(grad_in.astype(jnp.bfloat16))
        if tick_no < micro_total:
            outgoing = from_behind(grads_in[-1], "section", -1)
    shape_out = (1, micro_total, images.shape[1], images.shape[2], model_width)
    layer_out = jnp.stack(
        [
            jnp.where(is_first, outputs[micro_no], outputs[micro_no + 1])
            for micro_no in range(micro_total)
        ]
    ).reshape(shape_out)
    layer_in_grad = jnp.stack(
        [
            jnp.where(is_first, grads_in[micro_no + 1], grads_in[micro_no])
            for micro_no in range(micro_total)
        ]
    ).reshape(shape_out)
    acc_gain_one, acc_qkv, acc_out, acc_gain_two, acc_router, acc_up, acc_down = sums
    scattered = (
        lax.psum_scatter(
            acc_gain_one.astype(jnp.bfloat16), "shard", scatter_dimension=0, tiled=True
        ).astype(jnp.float32),
        lax.psum_scatter(
            acc_qkv.astype(jnp.bfloat16), "shard", scatter_dimension=0, tiled=True
        ).astype(jnp.float32),
        lax.psum_scatter(
            acc_out.astype(jnp.bfloat16), "shard", scatter_dimension=0, tiled=True
        ).astype(jnp.float32),
        lax.psum_scatter(
            acc_gain_two.astype(jnp.bfloat16), "shard", scatter_dimension=0, tiled=True
        ).astype(jnp.float32),
        lax.psum_scatter(
            acc_router.astype(jnp.bfloat16), "shard", scatter_dimension=0, tiled=True
        ).astype(jnp.float32),
    )
    summed = (
        lax.psum(scattered[0].astype(jnp.bfloat16), "expert").astype(jnp.float32),
        lax.psum(scattered[1].astype(jnp.bfloat16), "expert").astype(jnp.float32),
        lax.psum(scattered[2].astype(jnp.bfloat16), "expert").astype(jnp.float32),
        lax.psum(scattered[3].astype(jnp.bfloat16), "expert").astype(jnp.float32),
        lax.psum(scattered[4].astype(jnp.bfloat16), "expert").astype(jnp.float32),
    )
    up_grad, down_grad = (
        lax.psum_scatter(
            acc_up.astype(jnp.bfloat16), "shard", scatter_dimension=1, tiled=True
        ).astype(jnp.float32),
        lax.psum_scatter(
            acc_down.astype(jnp.bfloat16), "shard", scatter_dimension=1, tiled=True
        ).astype(jnp.float32),
    )
    return (
        layer_out,
        layer_in_grad,
        summed[0][None],
        summed[1][None],
        summed[2][None],
        summed[3][None],
        summed[4][None],
        up_grad[None],
        down_grad[None],
    )


def solution(mesh):
    in_specs = (
        P(None, ("expert", "shard"), None, None),
        P(None, ("expert", "shard"), None, None),
        P("section", "shard"),
        P("section", "shard", None),
        P("section", "shard", None),
        P("section", "shard"),
        P("section", "shard", None),
        P("section", "expert", "shard", None),
        P("section", "expert", "shard", None),
        P("section", None, ("expert", "shard"), None, None),
    )
    out_specs = (
        P("section", None, ("expert", "shard"), None, None),
        P("section", None, ("expert", "shard"), None, None),
        P("section", "shard"),
        P("section", "shard", None),
        P("section", "shard", None),
        P("section", "shard"),
        P("section", "shard", None),
        P("section", "expert", "shard", None),
        P("section", "expert", "shard", None),
    )
    return jax.shard_map(shards, mesh=mesh, in_specs=in_specs, out_specs=out_specs, check_vma=False)
```

profile of v0, /device:TPU:0, one launch (start us, length us, event | category | flops | bytes accessed | tf_op | source)
XLA Modules:
  0.0 790.1 jit_solution(425581261359813442)
XLA Ops:
  13.8 7.0 all-gather
  21.0 6.8 all-gather.3
  38.9 6.7 all-gather.4
  45.7 11.7 %all-gather.2 = bf16[1,512,512]{2,1,0:T(8,128)(2,1)S(1)} all-gather(bf16[1,128,512]{2,1,0:T(8,128)(2,1)S(1)} %copy-done.66), channel_id=4, replica_groups=mesh['section'=2,'expert'=16,'shard'=4] {'shard'}, dimensions={1}, use_global_device_ids=true | all-gather | bytes 655360 | tf_op jit(solution)/shard_map/all_gather | solution.py:320
  64.9 7.3 all-to-all-start
  72.3 11.1 %all-to-all-done = bf16[16,2,14,512]{3,1,2,0:T(2,128)(2,1)S(1)} async-done(((bf16[16,2,14,512]{3,1,2,0:T(2,128)(2,1)}), bf16[16,2,14,512]{3,1,2,0:T(2,128)(2,1)S(1)}, u32[]{:S(2)}, u32[]{:S(2)}) %all-to-all-start) | async-done | bytes 458784 | tf_op jit(solution)/shard_map/all_to_all | solution.py:58
  83.4 34.6 %all-gather.13.cloned.1.call-done = bf16[1,2,2048,512]{3,2,1,0:T(8,128)(2,1)} async-done(((bf16[1,2,512,512]{3,2,1,0:T(8,128)(2,1)}), bf16[1,2,2048,512]{3,2,1,0:T(8,128)(2,1)}) %all-gather.13.cloned.1.call-update) | async-done | bytes 4194320 | tf_op jit(solution)/shard_map/all_gather | solution.py:74
  118.0 5.9 fusion.171
  125.2 6.8 all-to-all-start.1
  132.2 11.1 %all-to-all-done.1 = bf16[16,2,14,512]{3,1,2,0:T(2,128)(2,1)S(1)} async-done(((bf16[16,2,14,512]{3,1,2,0:T(2,128)(2,1)}), bf16[16,2,14,512]{3,1,2,0:T(2,128)(2,1)S(1)}, u32[]{:S(2)}, u32[]{:S(2)}) %all-to-all-start.1) | async-done | bytes 458784 | tf_op jit(solution)/shard_map/all_to_all | solution.py:62
  145.9 3.3 collective-permute-start
  169.5 4.6 all-to-all-start.2
  180.9 2.9 all-to-all-done.2
  183.8 6.8 fusion.168
  193.0 4.5 all-to-all-start.3
  197.7 9.7 %all-to-all-done.3 = bf16[16,2,14,512]{3,1,2,0:T(2,128)(2,1)} async-done(((bf16[16,2,14,512]{3,1,2,0:T(2,128)(2,1)}), bf16[16,2,14,512]{3,1,2,0:T(2,128)(2,1)}, u32[]{:S(2)}, u32[]{:S(2)}) %all-to-all-start.3) | async-done | bytes 458784 | tf_op jit(solution)/shard_map/all_to_all | solution.py:62
  215.5 4.6 collective-permute-start.1
  228.9 2.8 convolution_convert_fusion
  234.2 4.3 broadcast_select_fusion
  254.1 4.4 all-to-all-start.4
  261.0 7.3 all-to-all-done.4
  268.3 4.2 all-to-all-start.6
  272.5 3.4 broadcast_select_fusion.3
  276.7 5.4 fusion.24
  282.3 6.7 fusion.38
  291.4 7.0 all-to-all-start.7
  298.4 6.8 fusion.165
  308.2 6.7 all-to-all-start.5
  331.5 2.7 convert_element_type.450
  334.2 3.0 multiply_reduce_fusion.14
  348.1 2.6 mul.803
  350.7 2.6 multiply_reduce_fusion.4
  359.1 7.7 all-to-all-start.8
  366.8 5.6 fusion.20
  372.4 4.2 all-to-all-done.8
  377.3 6.5 fusion.45
  386.3 3.6 all-to-all-start.9
  389.9 5.5 fusion.16
  395.4 4.1 all-to-all-done.9
  411.1 2.7 convert_element_type.466
  422.2 3.6 collective-permute-done.3
  428.4 2.6 mul.843
  444.5 4.2 all-to-all-start.10
  451.3 4.6 convolution_add_fusion.1
  455.9 2.6 all-to-all-done.10
  458.5 6.7 fusion.52
  467.7 4.5 all-to-all-start.11
  472.2 2.7 convolution_add_fusion.3
  476.3 5.7 all-to-all-done.11
  502.7 4.1 fusion.95
  507.2 6.2 fusion.284
  514.6 6.1 fusion.279
  520.7 36.2 %reduce-scatter.8.cloned.1.call-done = bf16[128,1536]{1,0:T(8,128)(2,1)} async-done(((bf16[512,1536]{1,0:T(8,128)(2,1)}), bf16[128,1536]{1,0:T(8,128)(2,1)}) %reduce-scatter.8.cloned.1.call-update) | async-done | bytes 393232 | tf_op jit(solution)/shard_map/reduce_scatter | solution.py:388
  557.0 9.6 %fusion.1 = bf16[2,2048,512]{2,1,0:T(8,128)(2,1)} fusion(f32[2,2048,512,1]{2,1,3,0:T(8,128)} %fusion.279, f32[2,2048,512,1]{2,1,3,0:T(8,128)} %fusion.284, bf16[16,2,14,2048]{3,0,2,1:T(8,128)(2,1)} %copy-done.133, bf16[16,2,14,512]{3,1,2,0:T(2,128)(2,1)S(1)} %copy-done.41), kind=kOutput, calls=%fused_computation.4 | convolution fusion | flops 945815552 | bytes 23265280 | tf_op jit(solution)/shard_map/secf,secd->efd/dot_general | solution.py:53
  566.9 7.0 fusion.102
  574.0 4.7 fusion.104
  578.7 9.0 %fusion = bf16[2,2048,512]{2,1,0:T(8,128)(2,1)} fusion(f32[2,2048,512,1]{2,1,3,0:T(8,128)} %fusion.104, f32[2,2048,512,1]{2,1,3,0:T(8,128)} %fusion.102, f32[2,16,14,2048]{3,1,2,0:T(8,128)S(1)} %copy-done.32, bf16[16,2,14,512]{3,1,2,0:T(2,128)(2,1)} %all-to-all-done.10), kind=kOutput, calls=%fused_computation.1 | convolution fusion | flops 954073088 | bytes 25100288 | tf_op jit(solution)/shard_map/secf,secd->efd/dot_general | solution.py:43
  601.0 7.5 all-reduce.7
  608.6 41.3 %all-reduce.5 = (bf16[1,128]{1,0:T(2,128)(2,1)S(1)}, bf16[1,128]{1,0:T(2,128)(2,1)S(1)}, bf16[1,128,32]{1,2,0:T(8,128)(2,1)S(1)}) all-reduce(bf16[1,128]{1,0:T(2,128)(2,1)S(1)} %dynamic-slice_bitcast_fusion.1, bf16[1,128]{1,0:T(2,128)(2,1)S(1)} %dynamic-slice_bitcast_fusion, ...), channel_id=1, replica_groups=mesh['section'=2,'expert'=16,'shard'=4] {'expert'}, use_global_device_ids=true, to_apply=%region_70.71 | all-reduce | flops 4352 | bytes 17408 | tf_op jit(solution)/shard_map/psum | solution.py:402
  651.5 21.5 %all-reduce.10.cloned.1.call-done = (bf16[1,128,1536]{2,1,0:T(8,128)(2,1)}, bf16[1,128,512]{2,1,0:T(8,128)(2,1)}) async-done(((bf16[1,128,1536]{2,1,0:T(8,128)(2,1)}, bf16[1,128,512]{2,1,0:T(8,128)(2,1)}), (bf16[1,128,1536]{2,1,0:T(8,128)(2,1)}, bf16[1,128,512]{2,1,0:T(8,128)(2,1)})) %all-reduce.10.cloned.1.call-update) | async-done | bytes 524304 | tf_op jit(solution)/shard_map/psum | solution.py:403
  676.6 50.1 %reduce-scatter.12.cloned.1.call-done = bf16[2,512,512]{2,1,0:T(8,128)(2,1)} async-done(((bf16[2,2048,512]{2,1,0:T(8,128)(2,1)}), bf16[2,512,512]{2,1,0:T(8,128)(2,1)}) %reduce-scatter.12.cloned.1.call-update) | async-done | bytes 1048592 | tf_op jit(solution)/shard_map/reduce_scatter | solution.py:409
  726.7 2.8 bitcast_convert_fusion.1
  729.6 50.8 %reduce-scatter.14.cloned.1.call-done = bf16[2,512,512]{2,1,0:T(8,128)(2,1)} async-done(((bf16[2,2048,512]{2,1,0:T(8,128)(2,1)}), bf16[2,512,512]{2,1,0:T(8,128)(2,1)}) %reduce-scatter.14.cloned.1.call-update) | async-done | bytes 1048592 | tf_op jit(solution)/shard_map/reduce_scatter | solution.py:412
  780.3 2.8 bitcast_convert_fusion
  (581 shorter events, 220.5 us)
Async XLA Ops:
  7.2 50.3 %all-gather.11.cloned.1.call-start = ((), (), s32[]{:S(2)}) async-start(), calls=%async_computation.21 | async-start | bytes 1966080 | tf_op jit(solution)/shard_map/all_gather | solution.py:319
  8.0 75.4 %all-gather.15.cloned.1.call-start = ((), (), s32[]{:S(2)}) async-start(), calls=%async_computation.23 | async-start | bytes 5242880 | tf_op jit(solution)/shard_map/all_gather | solution.py:75
  8.7 109.3 %all-gather.13.cloned.1.call-start = ((), (), s32[]{:S(2)}) async-start(), calls=%async_computation.22 | async-start | bytes 5242880 | tf_op jit(solution)/shard_map/all_gather | solution.py:74
  21.0 316.3 %copy-start.73 = (f32[200]{0:T(256)}, f32[200]{0:T(256)S(1)}, u32[]{:S(2)}) copy-start(f32[200]{0:T(256)S(1)} %div.174) | copy-start | bytes 2404
  27.9 104.1 %copy-start.83 = (s32[200,2]{0,1:T(2,128)}, s32[200,2]{0,1:T(2,128)S(1)}, u32[]{:S(2)}) copy-start(s32[200,2]{0,1:T(2,128)S(1)} %eq.235) | copy-start | bytes 4804
  31.4 117.8 %copy-start.101 = (s32[400]{0:T(512)}, s32[400]{0:T(512)S(1)}, u32[]{:S(2)}) copy-start(s32[400]{0:T(512)S(1)} %get-tuple-element.161) | copy-start | bytes 4804
  31.4 131.6 %copy-start.99 = (s32[400]{0:T(512)}, s32[400]{0:T(512)S(1)}, u32[]{:S(2)}) copy-start(s32[400]{0:T(512)S(1)} %get-tuple-element.160) | copy-start | bytes 4804
  45.6 355.6 %copy-start.48 = (bf16[1,512,32]{1,2,0:T(8,128)(2,1)}, bf16[1,512,32]{1,2,0:T(8,128)(2,1)S(1)}, u32[]{:S(2)}) copy-start(bf16[1,512,32]{1,2,0:T(8,128)(2,1)S(1)} %all-gather.4) | copy-start | bytes 98308
  62.2 61.7 %copy-start.90 = (f32[200]{0:T(256)}, f32[200]{0:T(256)S(1)}, u32[]{:S(2)}) copy-start(f32[200]{0:T(256)S(1)} %broadcast_multiply_fusion.17) | copy-start | bytes 2404
  62.4 61.5 %copy-start.115 = (f32[200]{0:T(256)}, f32[200]{0:T(256)S(1)}, u32[]{:S(2)}) copy-start(f32[200]{0:T(256)S(1)} %multiply_reduce_fusion.23) | copy-start | bytes 2404
  62.5 61.5 %copy-start.110 = (f32[200]{0:T(256)}, f32[200]{0:T(256)S(1)}, u32[]{:S(2)}) copy-start(f32[200]{0:T(256)S(1)} %add_rsqrt_fusion.5) | copy-start | bytes 2404
  62.7 61.3 %copy-start.22 = (bf16[200,512]{1,0:T(8,128)(2,1)}, bf16[200,512]{1,0:T(8,128)(2,1)S(1)}, u32[]{:S(2)}) copy-start(bf16[200,512]{1,0:T(8,128)(2,1)S(1)} %multiply_convert_fusion.11) | copy-start | bytes 614404
  64.9 18.5 %all-to-all-start = ((bf16[16,2,14,512]{3,1,2,0:T(2,128)(2,1)}), bf16[16,2,14,512]{3,1,2,0:T(2,128)(2,1)S(1)}, u32[]{:S(2)}, u32[]{:S(2)}) async-start(bf16[16,2,14,512]{3,1,2,0:T(2,128)(2,1)} %copy.461), calls=%async_computation | async-start | bytes 917504 | tf_op jit(solution)/shard_map/all_to_all | solution.py:58
  72.1 102.0 %copy-start.97 = (s32[400]{0:T(512)}, s32[400]{0:T(512)S(1)}, u32[]{:S(2)}) copy-start(s32[400]{0:T(512)S(1)} %multiply_add_fusion.3) | copy-start | bytes 4804
  83.4 40.6 %copy-start.39 = (bf16[16,2,14,512]{3,1,2,0:T(2,128)(2,1)}, bf16[16,2,14,512]{3,1,2,0:T(2,128)(2,1)S(1)}, u32[]{:S(2)}) copy-start(bf16[16,2,14,512]{3,1,2,0:T(2,128)(2,1)S(1)} %all-to-all-done) | copy-start | bytes 1376260
  125.2 18.0 %all-to-all-start.1 = ((bf16[16,2,14,512]{3,1,2,0:T(2,128)(2,1)}), bf16[16,2,14,512]{3,1,2,0:T(2,128)(2,1)S(1)}, u32[]{:S(2)}, u32[]{:S(2)}) async-start(bf16[16,2,14,512]{3,1,2,0:T(2,128)(2,1)} %copy.463), calls=%async_computation.1 | async-start | bytes 917504 | tf_op jit(solution)/shard_map/all_to_all | solution.py:62
  132.1 19.3 %copy-start.51 = (bf16[1,4,50,512]{3,1,2,0:T(4,128)(2,1)S(1)}, bf16[1,4,50,512]{3,1,2,0:T(4,128)(2,1)}, u32[]{:S(2)}) copy-start(bf16[1,4,50,512]{3,1,2,0:T(4,128)(2,1)} %get-tuple-element.108) | copy-start | bytes 614404
  132.1 19.3 %copy-start.94 = (f32[200]{0:T(256)}, f32[200]{0:T(256)S(1)}, u32[]{:S(2)}) copy-start(f32[200]{0:T(256)S(1)} %reduce_max.55) | copy-start | bytes 2404
  132.2 19.3 %copy-start.113 = (f32[200]{0:T(256)}, f32[200]{0:T(256)S(1)}, u32[]{:S(2)}) copy-start(f32[200]{0:T(256)S(1)} %fusion.350) | copy-start | bytes 2404
  132.2 20.0 %copy-start.37 = (bf16[200,512]{1,0:T(8,128)(2,1)S(1)}, bf16[200,512]{1,0:T(8,128)(2,1)}, u32[]{:S(2)}) copy-start(bf16[200,512]{1,0:T(8,128)(2,1)} %reshape_squeeze.4) | copy-start | bytes 614404
  145.9 6.3 collective-permute-start
  152.3 185.0 %copy-start.4 = (bf16[200,512]{1,0:T(8,128)(2,1)}, bf16[200,512]{1,0:T(8,128)(2,1)S(1)}, u32[]{:S(2)}) copy-start(bf16[200,512]{1,0:T(8,128)(2,1)S(1)} %get-tuple-element.100) | copy-start | bytes 614404
  152.3 185.0 %copy-start.71 = (f32[200]{0:T(256)}, f32[200]{0:T(256)S(1)}, u32[]{:S(2)}) copy-start(f32[200]{0:T(256)S(1)} %broadcast_multiply_fusion.16) | copy-start | bytes 2404
  159.7 17.5 %copy-start.88 = (f32[200]{0:T(256)}, f32[200]{0:T(256)S(1)}, u32[]{:S(2)}) copy-start(f32[200]{0:T(256)S(1)} %broadcast_multiply_fusion.15) | copy-start | bytes 2404
  160.0 19.8 %copy-start.116 = (f32[200]{0:T(256)}, f32[200]{0:T(256)S(1)}, u32[]{:S(2)}) copy-start(f32[200]{0:T(256)S(1)} %multiply_reduce_fusion.22) | copy-start | bytes 2404
  160.0 19.8 %copy-start.108 = (f32[200]{0:T(256)}, f32[200]{0:T(256)S(1)}, u32[]{:S(2)}) copy-start(f32[200]{0:T(256)S(1)} %add_rsqrt_fusion.3) | copy-start | bytes 2404
  160.1 20.6 %copy-start.24 = (bf16[200,512]{1,0:T(8,128)(2,1)}, bf16[200,512]{1,0:T(8,128)(2,1)S(1)}, u32[]{:S(2)}) copy-start(bf16[200,512]{1,0:T(8,128)(2,1)S(1)} %multiply_convert_fusion.10) | copy-start | bytes 614404
  160.2 19.7 %copy-start.45 = (bf16[400,448]{1,0:T(8,128)(2,1)S(1)}, bf16[400,448]{1,0:T(8,128)(2,1)}, u32[]{:S(2)}) copy-start(bf16[400,448]{1,0:T(8,128)(2,1)} %get-tuple-element.118) | copy-start | bytes 1075204
  169.5 14.4 %all-to-all-start.2 = ((bf16[16,2,14,512]{3,1,2,0:T(2,128)(2,1)}), bf16[16,2,14,512]{3,1,2,0:T(2,128)(2,1)}, u32[]{:S(2)}, u32[]{:S(2)}) async-start(bf16[16,2,14,512]{3,1,2,0:T(2,128)(2,1)} %copy.476), calls=%async_computation.2 | async-start | bytes 917504 | tf_op jit(solution)/shard_map/all_to_all | solution.py:58
  180.9 16.6 %copy-start.81 = (s32[200,2]{0,1:T(2,128)S(1)}, s32[200,2]{0,1:T(2,128)}, u32[]{:S(2)}) copy-start(s32[200,2]{0,1:T(2,128)} %eq.252) | copy-start | bytes 4804
  190.6 20.5 %copy-start.20 = (f32[200,512]{1,0:T(8,128)S(1)}, f32[200,512]{1,0:T(8,128)}, u32[]{:S(2)}) copy-start(f32[200,512]{1,0:T(8,128)} %copy-done.19) | copy-start | bytes 1228804
  193.0 27.2 %copy-start.95 = (f32[200]{0:T(256)S(1)}, f32[200]{0:T(256)}, u32[]{:S(2)}) copy-start(f32[200]{0:T(256)} %copy-done.94) | copy-start | bytes 2404
  193.0 28.1 %copy-start.100 = (s32[400]{0:T(512)S(1)}, s32[400]{0:T(512)}, u32[]{:S(2)}) copy-start(s32[400]{0:T(512)} %copy-done.99) | copy-start | bytes 4804
  193.0 28.2 %copy-start.102 = (s32[400]{0:T(512)S(1)}, s32[400]{0:T(512)}, u32[]{:S(2)}) copy-start(s32[400]{0:T(512)} %copy-done.101) | copy-start | bytes 4804
  193.0 14.4 %all-to-all-start.3 = ((bf16[16,2,14,512]{3,1,2,0:T(2,128)(2,1)}), bf16[16,2,14,512]{3,1,2,0:T(2,128)(2,1)}, u32[]{:S(2)}, u32[]{:S(2)}) async-start(bf16[16,2,14,512]{3,1,2,0:T(2,128)(2,1)} %copy.478), calls=%async_computation.3 | async-start | bytes 917504 | tf_op jit(solution)/shard_map/all_to_all | solution.py:62
  197.6 26.0 %copy-start.93 = (f32[200]{0:T(256)}, f32[200]{0:T(256)S(1)}, u32[]{:S(2)}) copy-start(f32[200]{0:T(256)S(1)} %reduce_max.57) | copy-start | bytes 2404
  197.6 25.9 %copy-start.112 = (f32[200]{0:T(256)}, f32[200]{0:T(256)S(1)}, u32[]{:S(2)}) copy-start(f32[200]{0:T(256)S(1)} %fusion.352) | copy-start | bytes 2404
  211.2 16.6 %copy-start.84 = (s32[200,2]{0,1:T(2,128)S(1)}, s32[200,2]{0,1:T(2,128)}, u32[]{:S(2)}) copy-start(s32[200,2]{0,1:T(2,128)} %copy-done.83) | copy-start | bytes 4804
  213.7 14.5 %copy-start.118 = (f32[200]{0:T(256)S(1)}, f32[200]{0:T(256)}, u32[]{:S(2)}) copy-start(f32[200]{0:T(256)} %copy-done.117) | copy-start | bytes 2404
  215.5 12.3 %collective-permute-start.1 = (bf16[200,512]{1,0:T(8,128)(2,1)S(1)}, bf16[200,512]{1,0:T(8,128)(2,1)}, u32[]{:S(2)}, u32[]{:S(2)}) collective-permute-start(bf16[200,512]{1,0:T(8,128)(2,1)S(1)} %get-tuple-element.89), channel_id=1, source_target_pairs={{0,64},{1,65},{2,66},{3,67},{4,68},{5,69},{6,70},{7,71},{8,72},{9,... | collective-permute-start | bytes 614408 | tf_op jit(solution)/shard_map/ppermute | solution.py:18
  227.8 92.6 %copy-start.61 = (bf16[200,32]{0,1:T(8,128)(2,1)}, bf16[200,32]{0,1:T(8,128)(2,1)S(1)}, u32[]{:S(2)}) copy-start(bf16[200,32]{0,1:T(8,128)(2,1)S(1)} %fusion.322) | copy-start | bytes 38404
  242.0 159.2 %copy-start.92 = (f32[200]{0:T(256)}, f32[200]{0:T(256)S(1)}, u32[]{:S(2)}) copy-start(f32[200]{0:T(256)S(1)} %broadcast_multiply_fusion.13) | copy-start | bytes 2404
  254.1 14.1 %all-to-all-start.4 = ((bf16[16,2,14,512]{3,1,2,0:T(2,128)(2,1)}), bf16[16,2,14,512]{3,1,2,0:T(2,128)(2,1)}, u32[]{:S(2)}, u32[]{:S(2)}) async-start(bf16[16,2,14,512]{3,1,2,0:T(2,128)(2,1)} %copy.490), calls=%async_computation.4 | async-start | bytes 917504 | tf_op jit(solution)/shard_map/all_to_all | solution.py:58
  268.3 14.0 %all-to-all-start.6 = ((bf16[16,2,14,512]{3,1,2,0:T(2,128)(2,1)}), bf16[16,2,14,512]{3,1,2,0:T(2,128)(2,1)}, u32[]{:S(2)}, u32[]{:S(2)}) async-start(bf16[16,2,14,512]{3,1,2,0:T(2,128)(2,1)} %copy.498), calls=%async_computation.6 | async-start | bytes 917504 | tf_op jit(solution)/shard_map/all_to_all | solution.py:58
  291.4 16.8 %all-to-all-start.7 = ((bf16[16,2,14,512]{3,1,2,0:T(2,128)(2,1)}), bf16[16,2,14,512]{3,1,2,0:T(2,128)(2,1)}, u32[]{:S(2)}, u32[]{:S(2)}) async-start(bf16[16,2,14,512]{3,1,2,0:T(2,128)(2,1)} %copy.501), calls=%async_computation.7 | async-start | bytes 917504 | tf_op jit(solution)/shard_map/all_to_all | solution.py:62
  305.2 15.2 %copy-start.89 = (f32[200]{0:T(256)S(1)}, f32[200]{0:T(256)}, u32[]{:S(2)}) copy-start(f32[200]{0:T(256)} %copy-done.88) | copy-start | bytes 2404
  305.2 15.2 %copy-start.91 = (f32[200]{0:T(256)S(1)}, f32[200]{0:T(256)}, u32[]{:S(2)}) copy-start(f32[200]{0:T(256)} %copy-done.90) | copy-start | bytes 2404
  305.2 15.2 %copy-start.109 = (f32[200]{0:T(256)S(1)}, f32[200]{0:T(256)}, u32[]{:S(2)}) copy-start(f32[200]{0:T(256)} %copy-done.108) | copy-start | bytes 2404
  305.2 15.2 %copy-start.111 = (f32[200]{0:T(256)S(1)}, f32[200]{0:T(256)}, u32[]{:S(2)}) copy-start(f32[200]{0:T(256)} %copy-done.110) | copy-start | bytes 2404
  305.2 16.1 %copy-start.125 = (f32[200]{0:T(256)S(1)}, f32[200]{0:T(256)}, u32[]{:S(2)}) copy-start(f32[200]{0:T(256)} %get-tuple-element.128) | copy-start | bytes 2404
  308.2 31.5 %all-to-all-start.5 = ((bf16[16,2,14,512]{3,1,2,0:T(2,128)(2,1)}), bf16[16,2,14,512]{3,1,2,0:T(2,128)(2,1)}, u32[]{:S(2)}, u32[]{:S(2)}) async-start(bf16[16,2,14,512]{3,1,2,0:T(2,128)(2,1)} %copy.492), calls=%async_computation.5 | async-start | bytes 917504 | tf_op jit(solution)/shard_map/all_to_all | solution.py:62
  338.3 7.8 collective-permute-start.2
  359.1 17.5 %all-to-all-start.8 = ((bf16[16,2,14,512]{3,1,2,0:T(2,128)(2,1)}), bf16[16,2,14,512]{3,1,2,0:T(2,128)(2,1)S(1)}, u32[]{:S(2)}, u32[]{:S(2)}) async-start(bf16[16,2,14,512]{3,1,2,0:T(2,128)(2,1)} %copy.513), calls=%async_computation.8 | async-start | bytes 917504 | tf_op jit(solution)/shard_map/all_to_all | solution.py:58
  386.3 13.3 %all-to-all-start.9 = ((bf16[16,2,14,512]{3,1,2,0:T(2,128)(2,1)}), bf16[16,2,14,512]{3,1,2,0:T(2,128)(2,1)S(1)}, u32[]{:S(2)}, u32[]{:S(2)}) async-start(bf16[16,2,14,512]{3,1,2,0:T(2,128)(2,1)} %copy.516), calls=%async_computation.9 | async-start | bytes 917504 | tf_op jit(solution)/shard_map/all_to_all | solution.py:62
  418.1 7.6 collective-permute-start.3
  444.5 14.0 %all-to-all-start.10 = ((bf16[16,2,14,512]{3,1,2,0:T(2,128)(2,1)}), bf16[16,2,14,512]{3,1,2,0:T(2,128)(2,1)}, u32[]{:S(2)}, u32[]{:S(2)}) async-start(bf16[16,2,14,512]{3,1,2,0:T(2,128)(2,1)} %copy.527), calls=%async_computation.10 | async-start | bytes 917504 | tf_op jit(solution)/shard_map/all_to_all | solution.py:58
  467.7 14.3 %all-to-all-start.11 = ((bf16[16,2,14,512]{3,1,2,0:T(2,128)(2,1)}), bf16[16,2,14,512]{3,1,2,0:T(2,128)(2,1)}, u32[]{:S(2)}, u32[]{:S(2)}) async-start(bf16[16,2,14,512]{3,1,2,0:T(2,128)(2,1)} %copy.530), calls=%async_computation.11 | async-start | bytes 917504 | tf_op jit(solution)/shard_map/all_to_all | solution.py:62
  472.2 48.5 %reduce-scatter.10.cloned.1.call-start = ((), (), s32[]{:S(2)}) async-start(), calls=%async_computation.18 | async-start | bytes 655360 | tf_op jit(solution)/shard_map/reduce_scatter | solution.py:391
  494.3 62.7 %reduce-scatter.8.cloned.1.call-start = ((), (), s32[]{:S(2)}) async-start(), calls=%async_computation.17 | async-start | bytes 1966080 | tf_op jit(solution)/shard_map/reduce_scatter | solution.py:388
  506.9 89.8 %reduce-scatter.16.cloned.1.call-start = ((), (), s32[]{:S(2)}) async-start(), calls=%async_computation.24 | async-start | bytes 163840
  514.5 42.5 %copy-start.41 = (bf16[16,2,14,512]{3,1,2,0:T(2,128)(2,1)S(1)}, bf16[16,2,14,512]{3,1,2,0:T(2,128)(2,1)}, u32[]{:S(2)}) copy-start(bf16[16,2,14,512]{3,1,2,0:T(2,128)(2,1)} %get-tuple-element.105) | copy-start | bytes 1376260
  514.5 158.6 %all-reduce.10.cloned.1.call-start = ((), (), s32[]{:S(2)}) async-start(), calls=%async_computation.25 | async-start | bytes 1048576 | tf_op jit(solution)/shard_map/psum | solution.py:403
  556.9 169.8 %reduce-scatter.12.cloned.1.call-start = ((), (), s32[]{:S(2)}) async-start(), calls=%async_computation.19 | async-start | bytes 5242880 | tf_op jit(solution)/shard_map/reduce_scatter | solution.py:409
  566.6 213.7 %reduce-scatter.14.cloned.1.call-start = ((), (), s32[]{:S(2)}) async-start(), calls=%async_computation.20 | async-start | bytes 5242880 | tf_op jit(solution)/shard_map/reduce_scatter | solution.py:412
  (95 other events, 514.5 us)
Sparse Core Ops, SparseCore 0:
  9.7 26.3 all-gather.10
  37.7 40.1 all-gather.14
  79.6 38.4 all-gather.12
  494.4 25.3 reduce-scatter.9
  522.5 34.4 reduce-scatter.7
  559.3 25.8 reduce-scatter.15
  588.7 84.2 all-reduce.9
  675.7 50.9 reduce-scatter.11
  729.6 50.7 reduce-scatter.13
where the time goes:
time: 802 us; the launch traced here: 790 us
  waiting for transfers between devices  261 us (33%)
  matrix products  183 us (23%)
  local copies, waits for them, and re-layouts  118 us (15%)
  blocking collectives  80.9 us (10%)
  starting transfers between devices  77 us (10%)
  other arithmetic  53.1 us (7%)
  between operations  17.3 us (2%)
    reduce_scatter x1, waiting for transfers between devices, shards(): lax.psum_scatter(acc_down.astype(jnp.bfloat16), 'shard', scatter_dimensio...  50.8 us
    reduce_scatter x1, waiting for transfers between devices, shards(): lax.psum_scatter(acc_up.astype(jnp.bfloat16), 'shard', scatter_dimension=...  50.1 us
    psum x1, blocking collectives, shards(): lax.psum(scattered[0].astype(jnp.bfloat16), 'expert').astype(jnp.float32)  41.3 us
    reduce_scatter x1, waiting for transfers between devices, shards(): lax.psum_scatter(acc_qkv.astype(jnp.bfloat16), 'shard', scatter_dimension...  36.2 us
    all_gather x1, waiting for transfers between devices, expert_forward(): lax.all_gather(up_local, 'shard', axis=1, tiled=True)  34.6 us
    all_to_all x6, starting transfers between devices, from_experts(): lax.all_to_all(values, 'expert', split_axis=0, concat_axis=0, tiled=True)  33.1 us
    all_to_all x6, starting transfers between devices, to_experts(): lax.all_to_all(values, 'expert', split_axis=0, concat_axis=0, tiled=True)  32.4 us
    all_to_all x6, waiting for transfers between devices, from_experts(): lax.all_to_all(values, 'expert', split_axis=0, concat_axis=0, tiled=True)  31.2 us
  transfers between devices with their start and end apart: 25, of which 18 were waited for; matrix products, arithmetic and copies ran while one was open for 24% of the time, Pallas kernels for 0%

commit v1 on v0

v1 whole, which is shorter than its diff:
```python
import jax
import jax.numpy as jnp
from jax import lax
from jax.experimental import pallas as pl
from jax.experimental.pallas import tpu as pltpu
from jax.sharding import PartitionSpec as P

HEADS = 8
HEAD_DIM = 64
TOPK = 2
SEQ = 50
ROWS = 200
T = 256
D = 512
EXPERTS = 32
SLOTS = 16
SHARED = 2176
WIDE = 1152
EPS = 1e-06
F32 = jnp.float32
BF16 = jnp.bfloat16
MESH = pl.DeviceIdType.MESH


def nn(a, b):
    return lax.dot_general(a, b, (((1,), (0,)), ((), ())), preferred_element_type=F32)


def nt(a, b):
    return lax.dot_general(a, b, (((1,), (1,)), ((), ())), preferred_element_type=F32)


def tn(a, b):
    return lax.dot_general(a, b, (((0,), (0,)), ((), ())), preferred_element_type=F32)


def iota(shape, dim):
    return lax.broadcasted_iota(jnp.int32, shape, dim).astype(F32)


def one(condition):
    return jnp.where(condition, 1.0, 0.0)


def normalize(values):
    shifted = values - jnp.mean(values, axis=-1, keepdims=True)
    inverse = lax.rsqrt(jnp.mean(shifted * shifted, axis=-1, keepdims=True) + EPS)
    return shifted * inverse, inverse


def norm_back(grad, normed, inverse):
    mean_grad = jnp.mean(grad, axis=-1, keepdims=True)
    mean_cross = jnp.mean(grad * normed, axis=-1, keepdims=True)
    return inverse * (grad - mean_grad - normed * mean_cross)


ROOT = 0.7978845608028654
CUBE = 0.044715


def gelu(x):
    return 0.5 * x * (1.0 + jnp.tanh(ROOT * (x + CUBE * x * x * x)))


def gelu_both(x):
    square = x * x
    bent = jnp.tanh(ROOT * x * (1.0 + CUBE * square))
    half = 0.5 * (1.0 + bent)
    slope = half + 0.5 * x * (1.0 - bent * bent) * (ROOT * (1.0 + 3.0 * CUBE * square))
    return x * half, slope


A2A_S, A2A_R = 0, 8
ROUTE_S, ROUTE_R = 16, 17
SH_S, SH_R, SHF_S, SHF_R = 18, 19, 21, 23
W_S, W_R, WF_S, WF_R = 25, 26, 28, 30
GWA_S, GWA_R, GWB_S, GWB_R = 32, 34, 36, 40
GSA_S, GSA_R, GSB_S, GSB_R = 41, 43, 45, 47
GSC_S, GSC_R, GSD_S, GSD_R = 49, 53, 54, 55
LO_S, LO_R, LI_S, LI_R = 56, 57, 58, 59
SEMS = 60


def kernel(
    x, cot, rt, shp, up, dn,
    lout, lig, ebuf, gd,
    w, sh, rts, rcol, bias, d_t, p_t,
    qkv_s, o_s, hid, pick, gat,
    rows_b, ret_b, g_b, dr_b, sbuf, acc,
    act_t, gp_t, dp_t, dqkv,
    gw, gwa, gs, gsa, gsb, gsc_s, gsc, gd_s, lo, li, sem,
):
    s, e, h = lax.axis_index("section"), lax.axis_index("expert"), lax.axis_index("shard")
    zh, c = lax.div(h, 2), lax.rem(h, 2)
    me = e * 2 + s
    sibling = (s, e, 2 * zh + 1 - c)
    other = (1 - s, e, h)

    def put(src, dst, send, recv, device):
        pltpu.make_async_remote_copy(
            src_ref=src, dst_ref=dst, send_sem=sem.at[send], recv_sem=sem.at[recv],
            device_id=device, device_id_type=MESH,
        ).start()

    def local(src, dst, recv):
        pltpu.make_async_copy(src, dst, sem.at[recv]).start()

    def wait(ref, number):
        pltpu.make_async_copy(ref, ref, sem.at[number]).wait()

    def put_or_local(own, src, dst, send, recv, device, here=None):
        @pl.when(own)
        def _():
            local(src, dst, recv if here is None else here)

        @pl.when(jnp.logical_not(own))
        def _():
            put(src, dst, send, recv, device)

    def wait_unless(own, ref, number):
        @pl.when(jnp.logical_not(own))
        def _():
            wait(ref, number)

    def a2a_start(phase, dst):
        local(sbuf.at[me], dst.at[me], A2A_R + phase)

        def step(i, carry):
            t = lax.rem(me + i, EXPERTS)
            put(sbuf.at[t], dst.at[me], A2A_S + phase, A2A_R + phase,
                (lax.rem(t, 2), lax.div(t, 2), h))
            return carry

        lax.fori_loop(1, EXPERTS, step, 0)

    def a2a_finish(phase, dst):
        wait(dst, A2A_R + phase)
        wait(sbuf.at[pl.ds(0, EXPERTS - 1)], A2A_S + phase)

    put(rt.at[1 - s], rts.at[s], ROUTE_S, ROUTE_R, other)
    rts[s] = rt[s]
    for layer in range(2):
        @pl.when(s == layer)
        def _():
            for to_s in range(2):
                for to_zh in range(2):
                    put_or_local(
                        jnp.logical_and(s == to_s, zh == to_zh),
                        shp, sh.at[layer, pl.ds(pl.multiple_of(h * 128, 128), 128)],
                        SH_S, SH_R + layer, (to_s, e, 2 * to_zh + c),
                    )

    def weights_start(layer):
        @pl.when(s == layer)
        def _():
            for to_s in range(2):
                for to_zh in range(2):
                    own = jnp.logical_and(s == to_s, zh == to_zh)
                    device = (to_s, e, 2 * to_zh + c)
                    put_or_local(own, up.at[to_s], w.at[layer, h, 0], W_S, W_R + layer, device)
                    put_or_local(own, dn.at[to_s], w.at[layer, h, 1], W_S, W_R + layer, device)

    weights_start(0)

    def image_of(index):
        return one(index >= 50) + one(index >= 100) + one(index >= 150) + one(index >= 200)

    bias[...] = jnp.where(
        image_of(iota((T, T), 0)) == image_of(iota((T, T), 1)), 0.0, -1e30
    )
    lane = iota((T, 128), 1)
    first_half = lane < 64.0
    half_row = iota((1, 128), 1)
    halves = (one(half_row < 64.0).astype(BF16), one(half_row >= 64.0).astype(BF16))
    sel_row, sel_lane = iota((8, 128), 0), iota((8, 128), 1)
    select = one(sel_lane == sel_row + 32.0) * one(sel_row < 2.0)
    select = select.astype(BF16)

    wait(rts.at[0], ROUTE_R)
    wait(rts.at[0], ROUTE_S)
    upper = one(iota((T, T), 0) < iota((T, T), 1)).astype(BF16)
    eye = one(sel_lane == sel_row).astype(BF16)
    for l in range(2):
        route = rts[l]
        number = iota((EXPERTS, T), 0)
        chosen = [one(route[k:k + 1] == number) for k in range(2)]
        earlier = nn((chosen[0] + chosen[1]).astype(BF16), upper)
        slot = [jnp.sum(earlier * chosen[k], axis=0, keepdims=True) for k in range(2)]
        slot_number = iota((EXPERTS * SLOTS, T), 0)
        for k in range(2):
            d_t[l, k] = one(slot_number == route[k:k + 1] * SLOTS + slot[k]).astype(BF16)
        row8 = iota((8, T), 0)
        listing = jnp.where(
            row8 == 0.0, route[0:1],
            jnp.where(row8 == 1.0, route[1:2],
                      jnp.where(row8 == 2.0, slot[0], jnp.where(row8 == 3.0, slot[1], 0.0))),
        )
        columns = tn(listing.astype(BF16), eye)
        rcol[l] = columns
        lane_number = iota((T, EXPERTS * SLOTS), 1)
        for k in range(2):
            target = columns[:, k:k + 1] * SLOTS + columns[:, 2 + k:3 + k]
            p_t[l, k] = one(lane_number == target).astype(BF16)

    def choices(l):
        columns = rcol[l]
        return [one(lane == columns[:, k:k + 1]) for k in range(2)]

    def gains(l):
        rows = nt(select, sh[l, :, 2048:2176])
        return rows[0:1], rows[1:2]

    def shared_forward(l):
        wait(sh.at[l, pl.ds(0, 256)], SH_R + l)
        for from_zh in range(2):
            part = sh.at[l, pl.ds(pl.multiple_of((2 * from_zh + c) * 128, 128), 128)]
            put(part, part, SHF_S + l, SHF_R + l, sibling)
        wait(sh.at[l, pl.ds(0, 256)], SHF_R + l)
        wait(sh.at[l, pl.ds(0, 256)], SHF_S + l)

    def weights_forward(l):
        wait(w.at[l, pl.ds(0, 2)], W_R + l)
        for from_zh in range(2):
            part = w.at[l, 2 * from_zh + c]
            put(part, part, WF_S + l, WF_R + l, sibling)

    def weights_finish(l):
        for number in (WF_R + l, WF_S + l):
            wait(w.at[l, pl.ds(0, 2)], number)

    def forward(l):
        rows_in = (x[...] if l == 0 else lo[0]).astype(F32)
        normed, _ = normalize(rows_in)
        shared_forward(l)
        gain_one, gain_two = gains(l)
        first_in = (normed * gain_one).astype(BF16)
        qkv_s[l] = nn(first_in, sh[l, :, 0:1536]).astype(BF16)
        for pair in range(4):
            at = pair * 128
            q = qkv_s[l, :, at:at + 128]
            k = qkv_s[l, :, 512 + at:640 + at]
            v = qkv_s[l, :, 1024 + at:1152 + at]
            outs = []
            for half in range(2):
                scores = nt(q * halves[half], k) * (HEAD_DIM ** -0.5) + bias[...]
                raised = jnp.exp(scores - jnp.max(scores, axis=-1, keepdims=True))
                chance = raised / jnp.sum(raised, axis=-1, keepdims=True)
                outs.append(nn(chance.astype(BF16), v))
            o_s[l, :, at:at + 128] = jnp.where(first_half, outs[0], outs[1]).astype(BF16)
        hidden = rows_in + nn(o_s[l], sh[l, :, 1536:2048])
        hid[l] = hidden
        normed, _ = normalize(hidden)
        second_in = (normed * gain_two).astype(BF16)
        sbuf[...] = nn(d_t[l, 0] + d_t[l, 1], second_in).astype(BF16).reshape(EXPERTS, SLOTS, D)
        a2a_start(2 * l, rows_b.at[l])
        logits = nn(second_in, sh[l, :, 2048:2176])
        picked = [jnp.sum(ch * logits, axis=1, keepdims=True) for ch in choices(l)]
        top = jnp.maximum(picked[0], picked[1])
        raised = [jnp.exp(value - top) for value in picked]
        total = raised[0] + raised[1]
        gate = [value / total for value in raised]
        gat[l] = jnp.where(lane == 0.0, gate[0], jnp.where(lane == 1.0, gate[1], 0.0))
        weights_forward(l)
        a2a_finish(2 * l, rows_b.at[l])
        weights_finish(l)
        acc[...] = jnp.zeros_like(acc)

        def piece(j, carry):
            before = nt(rows_b[l].reshape(EXPERTS * SLOTS, D), w[l, j, 0])
            acc[...] += nn(gelu(before).astype(BF16), w[l, j, 1])
            return carry

        lax.fori_loop(0, 4, piece, 0)
        sbuf[...] = acc[...].astype(BF16).reshape(EXPERTS, SLOTS, D)
        a2a_start(2 * l + 1, ret_b.at[l])
        a2a_finish(2 * l + 1, ret_b.at[l])
        returned = ret_b[l].reshape(EXPERTS * SLOTS, D)
        result = hid[l]
        for k in range(2):
            mine = nn(p_t[l, k], returned)
            pick[l, k] = mine.astype(BF16)
            result = result + gat[l, :, k:k + 1] * mine
        lo[l] = result.astype(BF16)

    def gw_a(l):
        for to_zh in range(2):
            put(gw.at[2 * to_zh + 1 - c], gwa.at[l, to_zh], GWA_S + l, GWA_R + l, sibling)

    def gw_b(l):
        wait(gwa.at[l], GWA_R + l)
        for to_zh in range(2):
            j = 2 * to_zh + c
            own = jnp.logical_and(s == l, zh == to_zh)
            gw[j] = (gw[j].astype(F32) + gwa[l, to_zh].astype(F32)).astype(BF16)
            send = GWB_S + 2 * l + to_zh
            put_or_local(own, gw.at[j], ebuf.at[2 * s + zh], send, GWB_R, (l, e, j), send)

    def gw_sent(l):
        wait(gwa.at[l], GWA_S + l)
        for to_zh in range(2):
            wait(gw.at[0], GWB_S + 2 * l + to_zh)

    def gs_a(l):
        for to_zh in range(2):
            put(gs.at[l, 2 * to_zh + 1 - c], gsa.at[l, to_zh], GSA_S + l, GSA_R + l, sibling)

    def peers(step):
        def body(i, carry):
            step(lax.rem(e + i, 16))
            return carry

        lax.fori_loop(1, 16, body, 0)

    def gs_b(l):
        wait(gsa.at[l], GSA_R + l)
        for to_zh in range(2):
            j = 2 * to_zh + c
            gs[l, j] = (gs[l, j].astype(F32) + gsa[l, to_zh].astype(F32)).astype(BF16)

        def part(to_zh, to_e):
            return gs.at[l, 2 * to_zh + c, pl.ds(pl.multiple_of(to_e * 16, 16), 16)]

        def step(to_e):
            for to_zh in range(2):
                put(part(to_zh, to_e), gsb.at[l, e, to_zh], GSB_S + l, GSB_R + l, (s, to_e, h))

        for to_zh in range(2):
            local(part(to_zh, e), gsb.at[l, e, to_zh], GSB_R + l)
        peers(step)

    def gs_c(l):
        wait(gsb.at[l], GSB_R + l)
        total = gsb[l, 0].astype(F32)
        for source in range(1, 16):
            total = total + gsb[l, source].astype(F32)
        gsc_s[l] = total.astype(BF16)
        for to_zh in range(2):
            own = jnp.logical_and(s == l, zh == to_zh)
            put_or_local(own, gsc_s.at[l, to_zh], gsc.at[2 * s + zh], GSC_S + 2 * l + to_zh, GSC_R,
                         (l, e, 2 * to_zh + c))

    def gs_d():
        wait(gsc, GSC_R)
        total = gsc[0].astype(F32)
        for source in range(1, 4):
            total = total + gsc[source].astype(F32)
        gd_s[...] = total.astype(BF16)
        local(gd_s, gd.at[e], GSD_R)
        peers(lambda to_e: put(gd_s, gd.at[e], GSD_S, GSD_R, (s, to_e, h)))

    def gs_sent(l):
        wait(gsa.at[l], GSA_S + l)
        wait(gsb.at[l, pl.ds(0, 15)], GSB_S + l)
        for to_zh in range(2):
            wait_unless(jnp.logical_and(s == l, zh == to_zh), gsc_s.at[l, to_zh], GSC_S + 2 * l + to_zh)

    def backward(l, grad_out, hook_one, hook_two):
        gate = [gat[l, :, k:k + 1] for k in range(2)]
        grad_gate = [
            jnp.sum(grad_out * pick[l, k].astype(F32), axis=-1, keepdims=True) for k in range(2)
        ]
        copies = [(gate[k] * grad_out).astype(BF16) for k in range(2)]
        sent = nn(d_t[l, 0], copies[0]) + nn(d_t[l, 1], copies[1])
        sbuf[...] = sent.astype(BF16).reshape(EXPERTS, SLOTS, D)
        a2a_start(4 + 2 * l, g_b.at[l])

        def again(j, carry):
            before = nt(w[l, j, 0], rows_b[l].reshape(EXPERTS * SLOTS, D))
            active, slope = gelu_both(before)
            act_t[j] = active.astype(BF16)
            gp_t[j] = slope
            return carry

        lax.fori_loop(0, 4, again, 0)
        hook_one()
        a2a_finish(4 + 2 * l, g_b.at[l])
        acc[...] = jnp.zeros_like(acc)

        def back(j, carry):
            grad_active = nt(w[l, j, 1], g_b[l].reshape(EXPERTS * SLOTS, D))
            grad_before = (grad_active * gp_t[j]).astype(BF16)
            dp_t[j] = grad_before
            acc[...] += tn(grad_before, w[l, j, 0])
            return carry

        lax.fori_loop(0, 4, back, 0)
        sbuf[...] = acc[...].astype(BF16).reshape(EXPERTS, SLOTS, D)
        a2a_start(5 + 2 * l, dr_b.at[l])

        def weight_grads(j, carry):
            gw[j, 1] = nn(act_t[j], g_b[l].reshape(EXPERTS * SLOTS, D)).astype(BF16)
            gw[j, 0] = nn(dp_t[j], rows_b[l].reshape(EXPERTS * SLOTS, D)).astype(BF16)
            return carry

        lax.fori_loop(0, 4, weight_grads, 0)
        gw_a(l)
        total = gate[0] * grad_gate[0] + gate[1] * grad_gate[1]
        chosen = choices(l)
        grad_logits = (
            chosen[0] * (gate[0] * (grad_gate[0] - total))
            + chosen[1] * (gate[1] * (grad_gate[1] - total))
        ).astype(BF16)
        hook_two()
        a2a_finish(5 + 2 * l, dr_b.at[l])
        gain_one, gain_two = gains(l)
        returned = dr_b[l].reshape(EXPERTS * SLOTS, D)
        grad_second = nn(p_t[l, 0] + p_t[l, 1], returned) + nt(grad_logits, sh[l, :, 2048:2176])
        normed, inverse = normalize(hid[l])
        second_in = (normed * gain_two).astype(BF16)
        gain_two_grad = jnp.sum(grad_second * normed, axis=0, keepdims=True)
        grad_hidden = grad_out + norm_back(grad_second * gain_two, normed, inverse)
        grad_mixed = grad_hidden.astype(BF16)
        router_grad = tn(second_in, grad_logits)
        grad_heads = nt(grad_mixed, sh[l, :, 1536:2048]).astype(BF16)
        for j in range(4):
            gs[l, j, 128:256, 384:896] = tn(
                o_s[l, :, j * 128:(j + 1) * 128], grad_mixed
            ).astype(BF16)
        for pair in range(4):
            at = pair * 128
            q = qkv_s[l, :, at:at + 128]
            k = qkv_s[l, :, 512 + at:640 + at]
            v = qkv_s[l, :, 1024 + at:1152 + at]
            do = grad_heads[:, at:at + 128]
            grads = []
            for half in range(2):
                scores = nt(k, q * halves[half]) * (HEAD_DIM ** -0.5) + bias[...]
                raised = jnp.exp(scores - jnp.max(scores, axis=0, keepdims=True))
                chance = raised / jnp.sum(raised, axis=0, keepdims=True)
                grad_value = nn(chance.astype(BF16), do)
                grad_chance = nt(v, do * halves[half])
                cross = jnp.sum(chance * grad_chance, axis=0, keepdims=True)
                grad_scores = (chance * (grad_chance - cross)).astype(BF16)
                grad_key = nn(grad_scores, q) * (HEAD_DIM ** -0.5)
                grad_query = tn(grad_scores, k) * (HEAD_DIM ** -0.5)
                grads.append((grad_query, grad_key, grad_value))
            for part in range(3):
                both = jnp.where(first_half, grads[0][part], grads[1][part])
                dqkv[:, part * 512 + at:part * 512 + at + 128] = both.astype(BF16)
        rows_in = (x[...] if l == 0 else lo[0]).astype(F32)
        normed, inverse = normalize(rows_in)
        first_in = (normed * gain_one).astype(BF16)
        grad_first = nt(dqkv[...], sh[l, :, 0:1536])
        gain_one_grad = jnp.sum(grad_first * normed, axis=0, keepdims=True)
        grad_in = grad_hidden + norm_back(grad_first * gain_one, normed, inverse)
        li[l] = grad_in.astype(BF16)
        row8 = iota((8, D), 0)
        both = jnp.where(row8 == 0.0, gain_one_grad, jnp.where(row8 == 1.0, gain_two_grad, 0.0))
        narrow = (router_grad + tn(both.astype(BF16), select)).astype(BF16)
        for j in range(4):
            part = tn(first_in[:, j * 128:(j + 1) * 128], dqkv[...]).astype(BF16)
            gs[l, j, 0:128, :] = part[:, 0:WIDE]
            gs[l, j, 128:256, 0:384] = part[:, WIDE:1536]
            gs[l, j, 128:256, 896:1024] = narrow[j * 128:(j + 1) * 128]
            gs[l, j, 128:256, 1024:1152] = jnp.zeros((128, 128), BF16)
        gs_a(l)

    def exchange(mine, out, send, recv):
        local(mine.at[s], out.at[s], recv)
        put(mine.at[1 - s], out.at[s], send, recv, other)

    def nothing():
        return None

    forward(0)
    weights_start(1)
    forward(1)
    exchange(lo, lout, LO_S, LO_R)
    backward(1, cot[...].astype(F32), nothing, nothing)

    def first_hook():
        gw_b(1)
        gs_b(1)

    def second_hook():
        gs_c(1)

    def before_layer_zero():
        first_hook()
        gw_sent(1)

    backward(0, li[1].astype(F32), before_layer_zero, second_hook)
    exchange(li, lig, LI_S, LI_R)
    gw_b(0)
    gs_b(0)
    gs_c(0)
    gs_d()
    gw_sent(0)
    gs_sent(1)
    gs_sent(0)
    wait(sh.at[0, pl.ds(0, 384)], SH_S)
    wait(w.at[0, pl.ds(0, 3)], W_S)
    wait(gd.at[pl.ds(0, 15)], GSD_S)
    wait(gd, GSD_R)
    for out, send, recv in ((lout, LO_S, LO_R), (lig, LI_S, LI_R)):
        wait(out, recv)
        wait(out.at[0], send)
    wait(ebuf.at[pl.ds(0, 3)], GWB_R)


def shards(
    images, cotangent, ln1_gain, qkv_weight, out_weight, ln2_gain, router_weight,
    up_weight, down_weight, routes,
):
    section = lax.axis_index("section")
    pad = ((0, T - ROWS), (0, 0))
    x = jnp.pad(lax.dynamic_index_in_dim(images, section, 0, False).reshape(ROWS, D), pad)
    cot = jnp.pad(lax.dynamic_index_in_dim(cotangent, section, 0, False).reshape(ROWS, D), pad)
    rt = jnp.swapaxes(routes[0].reshape(2, ROWS, TOPK), 1, 2).astype(F32)
    rt = jnp.pad(rt, ((0, 0), (0, 6), (0, T - ROWS)), constant_values=-1.0)
    shp = jnp.concatenate(
        [qkv_weight[0], out_weight[0], router_weight[0], ln1_gain[0][:, None],
         ln2_gain[0][:, None], jnp.zeros((128, 94), BF16)], axis=1,
    )
    vmem, anywhere = pl.BlockSpec(memory_space=pltpu.VMEM), pl.BlockSpec(memory_space=pl.ANY)
    slots = (2, EXPERTS, SLOTS, D)
    scratch = [
        pltpu.VMEM((2, 4, 2, 512, D), BF16),
        pltpu.VMEM((2, D, SHARED), BF16),
        pltpu.VMEM((2, 8, T), F32), pltpu.VMEM((2, T, 128), F32),
        pltpu.VMEM((T, T), F32),
        pltpu.VMEM((2, 2, EXPERTS * SLOTS, T), BF16), pltpu.VMEM((2, 2, T, EXPERTS * SLOTS), BF16),
        pltpu.VMEM((2, T, 3 * D), BF16), pltpu.VMEM((2, T, D), BF16),
        pltpu.VMEM((2, T, D), F32), pltpu.VMEM((2, 2, T, D), BF16),
        pltpu.VMEM((2, T, 128), F32),
        pltpu.VMEM(slots, BF16), pltpu.VMEM(slots, BF16),
        pltpu.VMEM(slots, BF16), pltpu.VMEM(slots, BF16),
        pltpu.VMEM(slots[1:], BF16), pltpu.VMEM((EXPERTS * SLOTS, D), F32),
        pltpu.VMEM((4, 512, 512), BF16), pltpu.VMEM((4, 512, 512), F32),
        pltpu.VMEM((4, 512, 512), BF16), pltpu.VMEM((T, 3 * D), BF16),
        pltpu.VMEM((4, 2, 512, D), BF16), pltpu.VMEM((2, 2, 2, 512, D), BF16),
        pltpu.VMEM((2, 4, 256, WIDE), BF16), pltpu.VMEM((2, 2, 256, WIDE), BF16),
        pltpu.VMEM((2, 16, 2, 16, WIDE), BF16),
        pltpu.VMEM((2, 2, 16, WIDE), BF16), pltpu.VMEM((4, 16, WIDE), BF16),
        pltpu.VMEM((16, WIDE), BF16),
        pltpu.VMEM((2, T, D), BF16), pltpu.VMEM((2, T, D), BF16),
        pltpu.SemaphoreType.DMA((SEMS,)),
    ]
    lout, lig, ebuf, gd = pl.pallas_call(
        kernel,
        out_shape=(
            jax.ShapeDtypeStruct((2, T, D), BF16),
            jax.ShapeDtypeStruct((2, T, D), BF16),
            jax.ShapeDtypeStruct((4, 2, 512, D), BF16),
            jax.ShapeDtypeStruct((16, 16, WIDE), BF16),
        ),
        in_specs=[vmem, vmem, vmem, anywhere, anywhere, anywhere],
        out_specs=(anywhere,) * 4,
        scratch_shapes=scratch,
        compiler_params=pltpu.CompilerParams(
            has_side_effects=True, vmem_limit_bytes=63 * 1024 * 1024
        ),
    )(x, cot, rt, shp, up_weight[0], down_weight[0])
    shape_out = (1, 2) + images.shape[1:]
    layer_out = lout[:, :ROWS].reshape(shape_out)
    layer_in_grad = lig[:, :ROWS].reshape(shape_out)
    wide = ebuf.astype(F32)
    sums = (wide[0::2] + wide[1::2])
    gathered = gd.reshape(256, WIDE)
    flat = jnp.concatenate([gathered[:128], gathered[128:]], axis=1).astype(F32)
    return (
        layer_out,
        layer_in_grad,
        flat[:, 2080][None],
        flat[:, 0:1536][None],
        flat[:, 1536:2048][None],
        flat[:, 2081][None],
        flat[:, 2048:2080][None],
        sums[:, 0][None],
        sums[:, 1][None],
    )


def solution(mesh):
    in_specs = (
        P(None, ("expert", "shard"), None, None),
        P(None, ("expert", "shard"), None, None),
        P("section", "shard"),
        P("section", "shard", None),
        P("section", "shard", None),
        P("section", "shard"),
        P("section", "shard", None),
        P("section", "expert", "shard", None),
        P("section", "expert", "shard", None),
        P("section", None, ("expert", "shard"), None, None),
    )
    out_specs = (
        P("section", None, ("expert", "shard"), None, None),
        P("section", None, ("expert", "shard"), None, None),
        P("section", "shard"),
        P("section", "shard", None),
        P("section", "shard", None),
        P("section", "shard"),
        P("section", "shard", None),
        P("section", "expert", "shard", None),
        P("section", "expert", "shard", None),
    )
    return jax.shard_map(shards, mesh=mesh, in_specs=in_specs, out_specs=out_specs, check_vma=False)
```

time: 802 us -> 356 us (0.44); the launches traced: 790 us -> 355 us
  Pallas kernels: 0 us -> 333 us
  waiting for transfers between devices: 261 us -> 0 us
  matrix products: 183 us -> 0 us
  local copies, waits for them, and re-layouts: 118 us -> 14.6 us
  blocking collectives: 80.9 us -> 0 us
  starting transfers between devices: 77 us -> 0 us
  other arithmetic: 53.1 us -> 6.63 us
  between operations: 17.3 us -> 0.78 us
    pallas_call x0 -> x1, Pallas kernels: none -> 333 us  [shards(): pl.pallas_call(kernel, out_shape=(jax.ShapeDtypeStruct((2, T, D), BF16),...]
    dot_general x78 -> x0, matrix products: 183 us -> none  [the longest x3 22 us: expert_grads(): jnp.einsum('secf,secd->efd', grad_before, inputs, preferred_element_type=...]
    reduce_scatter x4 -> x0, waiting for transfers between devices: 137 us -> none  [the longest x1 50.8 us: shards(): lax.psum_scatter(acc_down.astype(jnp.bfloat16), 'shard', scatter_dimensio...]
    all_to_all x12 -> x0, starting transfers between devices: 65.6 us -> none  [the longest x6 33.1 us: from_experts(): lax.all_to_all(values, 'expert', split_axis=0, concat_axis=0, tiled=True)]
    all_to_all x12 -> x0, waiting for transfers between devices: 59.5 us -> none  [the longest x6 31.2 us: from_experts(): lax.all_to_all(values, 'expert', split_axis=0, concat_axis=0, tiled=True)]
    reshape x32 -> x2, local copies, waits for them, and re-layouts: 46 us -> 0.12 us  [the longest x1 0.06 us: shards(): lax.dynamic_index_in_dim(cotangent, section, 0, False).reshape(ROWS, D)]
    psum x1 -> x0, blocking collectives: 41.3 us -> none  [shards(): lax.psum(scattered[0].astype(jnp.bfloat16), 'expert').astype(jnp.float32)]
    all_gather x3 -> x0, waiting for transfers between devices: 34.6 us -> none  [the longest x1 34.6 us: expert_forward(): lax.all_gather(up_local, 'shard', axis=1, tiled=True)]
  transfers between devices with their start and end apart: 25 -> 0, of which waited for: 18 -> 0; matrix products, arithmetic and copies ran while one was open for 24% -> 0% of each run, Pallas kernels for 0% -> 0%
where the time goes in v1:
time: 356 us; the launch traced here: 355 us
  Pallas kernels  333 us (94%)
  local copies, waits for them, and re-layouts  14.6 us (4%)
  other arithmetic  6.63 us (2%)
    pallas_call x1, Pallas kernels, shards(): pl.pallas_call(kernel, out_shape=(jax.ShapeDtypeStruct((2, T, D), BF16),...  333 us

profile of v1, /device:TPU:0, one launch (start us, length us, event | category | flops | bytes accessed | tf_op | source)
XLA Modules:
  0.0 355.2 jit_solution(12220987435997723344)
XLA Ops:
  0.6 0.0 copy-start.3
  0.7 0.0 copy-start.1
  0.7 0.8 convert_element_type.18
  1.4 0.1 convert_element_type.19
  1.5 0.6 pad.13.rt
  2.1 0.8 copy.44
  2.9 0.8 copy.45
  3.7 0.8 copy.43
  4.5 1.2 constant_dynamic-slice_fusion
  5.7 0.1 reshape.37
  5.8 0.7 pad.12.cot
  6.6 0.1 reshape.36
  6.6 0.7 pad.11.x
  7.4 0.0 copy-done.3
  7.4 0.0 copy-done.1
  7.4 1.0 concatenate.6.shp
  8.4 333.2 %shard_map.169 = (bf16[2,256,512]{2,1,0:T(8,128)(2,1)}, bf16[2,256,512]{2,1,0:T(8,128)(2,1)}, bf16[4,2,512,512]{3,2,1,0:T(8,128)(2,1)}, bf16[16,16,1152]{2,1,0:T(8,128)(2,1)}) custom-call(bf16[256,512]{1,0:T(8,128)(2,1)} %pad.11.x, bf16[256,512]{1,0:T(8,128)(2,1)} %pad.12.cot, f32[2,8,256]{2,1,0:T(8,128)} %pad.13.rt, bf16[128,2176]{1,0:T(8,128)(2,1)} %concatenate.6.shp, ...), custom_call_target="tpu_custom_call" | custom-call | tf_op jit(solution)/shard_map/pallas_call | solution.py:539
  341.6 0.0 copy-start.2
  341.6 1.1 slice.45
  342.7 0.0 copy-start
  342.7 0.3 copy.46
  343.0 0.9 copy.48
  343.9 0.0 copy-done.2
  344.0 0.3 copy.47
  344.3 0.9 copy.49
  345.2 0.0 copy-done
  345.3 0.7 convert_reduce_fusion
  346.0 0.7 copy.50
  346.7 0.7 convert_bitcast_fusion
  347.4 0.1 maximum_convert_fusion
  347.5 1.0 slice_bitcast_fusion.2
  348.4 3.3 convert_element_type.22
  351.8 1.0 slice_add_fusion
  352.8 2.4 slice_bitcast_fusion
  (7 shorter events, 0.2 us)
Async XLA Ops:
  0.6 6.7 %copy-start.3 = (bf16[1,128,512]{2,1,0:T(8,128)(2,1)S(1)}, bf16[1,128,512]{2,1,0:T(8,128)(2,1)}, u32[]{:S(2)}) copy-start(bf16[1,128,512]{2,1,0:T(8,128)(2,1)} %param.14) | copy-start | bytes 393220
  0.7 6.7 %copy-start.1 = (bf16[1,128,1536]{2,1,0:T(8,128)(2,1)S(1)}, bf16[1,128,1536]{2,1,0:T(8,128)(2,1)}, u32[]{:S(2)}) copy-start(bf16[1,128,1536]{2,1,0:T(8,128)(2,1)} %param.13) | copy-start | bytes 1179652
  341.6 2.4 copy-start.2
  342.7 2.5 copy-start

commit v2 on v1

--- a/solution.py
+++ b/solution.py
@@ -74,16 +74,17 @@
 ROUTE_S, ROUTE_R = 16, 17
 SH_S, SH_R, SHF_S, SHF_R = 18, 19, 21, 23
 W_S, W_R, WF_S, WF_R = 25, 26, 28, 30
-GWA_S, GWA_R, GWB_S, GWB_R = 32, 34, 36, 40
-GSA_S, GSA_R, GSB_S, GSB_R = 41, 43, 45, 47
-GSC_S, GSC_R, GSD_S, GSD_R = 49, 53, 54, 55
-LO_S, LO_R, LI_S, LI_R = 56, 57, 58, 59
-SEMS = 60
+GWA_S, GWA_R, GWB_S, GWB_R = 32, 36, 40, 44
+GSA_S, GSA_R, GSB_S, GSB_R = 46, 48, 50, 52
+GSC_S, GSC_R, GSD_S, GSD_R = 54, 58, 59, 60
+LO_S, LO_R, LI_S, LI_R = 61, 62, 63, 64
+SHX_S, SHX_R = 65, 67
+SEMS = 69
 
 
 def kernel(
     x, cot, rt, shp, up, dn,
-    lout, lig, ebuf, gd,
+    lout, lig, eb_up0, eb_up1, eb_dn0, eb_dn1, gd,
     w, sh, rts, rcol, bias, d_t, p_t,
     qkv_s, o_s, hid, pick, gat,
     rows_b, ret_b, g_b, dr_b, sbuf, acc,
@@ -137,30 +138,21 @@
         wait(dst, A2A_R + phase)
         wait(sbuf.at[pl.ds(0, EXPERTS - 1)], A2A_S + phase)
 
-    put(rt.at[1 - s], rts.at[s], ROUTE_S, ROUTE_R, other)
-    rts[s] = rt[s]
-    for layer in range(2):
-        @pl.when(s == layer)
-        def _():
-            for to_s in range(2):
-                for to_zh in range(2):
-                    put_or_local(
-                        jnp.logical_and(s == to_s, zh == to_zh),
-                        shp, sh.at[layer, pl.ds(pl.multiple_of(h * 128, 128), 128)],
-                        SH_S, SH_R + layer, (to_s, e, 2 * to_zh + c),
-                    )
-
-    def weights_start(layer):
-        @pl.when(s == layer)
-        def _():
-            for to_s in range(2):
-                for to_zh in range(2):
-                    own = jnp.logical_and(s == to_s, zh == to_zh)
-                    device = (to_s, e, 2 * to_zh + c)
-                    put_or_local(own, up.at[to_s], w.at[layer, h, 0], W_S, W_R + layer, device)
-                    put_or_local(own, dn.at[to_s], w.at[layer, h, 1], W_S, W_R + layer, device)
-
-    weights_start(0)
+    barrier = pltpu.get_barrier_semaphore()
+
+    def greet(i, carry):
+        t = lax.rem(me + i, EXPERTS)
+        pl.semaphore_signal(
+            barrier, inc=1, device_id=(lax.rem(t, 2), lax.div(t, 2), h), device_id_type=MESH
+        )
+        return carry
+
+    lax.fori_loop(1, EXPERTS, greet, 0)
+    for to_s in range(2):
+        for i in range(1, 4):
+            pl.semaphore_signal(
+                barrier, inc=1, device_id=(to_s, e, lax.rem(h + i, 4)), device_id_type=MESH
+            )
 
     def image_of(index):
         return one(index >= 50) + one(index >= 100) + one(index >= 150) + one(index >= 200)
@@ -175,7 +167,69 @@
     sel_row, sel_lane = iota((8, 128), 0), iota((8, 128), 1)
     select = one(sel_lane == sel_row + 32.0) * one(sel_row < 2.0)
     select = select.astype(BF16)
-
+    rts[s] = rt[s]
+    pl.semaphore_wait(barrier, EXPERTS - 1 + 6)
+
+    put(rt.at[1 - s], rts.at[s], ROUTE_S, ROUTE_R, other)
+    own_rows = pl.ds(pl.multiple_of(h * 128, 128), 128)
+    own_columns = pl.ds(pl.multiple_of(e * 128, 128), 128)
+    for layer in range(2):
+        @pl.when(s == layer)
+        def _():
+            for to_s in range(2):
+                for to_zh in range(2):
+                    for columns in (own_columns, pl.ds(2048, 128)):
+                        put_or_local(
+                            jnp.logical_and(s == to_s, zh == to_zh),
+                            shp.at[:, columns], sh.at[layer, own_rows, columns],
+                            SH_S, SH_R + layer, (to_s, e, 2 * to_zh + c),
+                        )
+
+    def weights_start(layer, sections):
+        @pl.when(s == layer)
+        def _():
+            for to_s in sections:
+                for to_zh in range(2):
+                    own = jnp.logical_and(s == to_s, zh == to_zh)
+                    device = (to_s, e, 2 * to_zh + c)
+                    put_or_local(own, up.at[to_s], w.at[layer, h, 0], W_S, W_R + layer, device)
+                    put_or_local(own, dn.at[to_s], w.at[layer, h, 1], W_S, W_R + layer, device)
+
+    weights_start(0, (0, 1))
+    weights_start(1, (0,))
+
+    def peers(step):
+        def body(i, carry):
+            step(lax.rem(e + i, 16))
+            return carry
+
+        lax.fori_loop(1, 16, body, 0)
+
+    def shared_part(l, from_zh, columns):
+        rows = pl.ds(pl.multiple_of((2 * from_zh + c) * 128, 128), 128)
+        return sh.at[l, rows, columns]
+
+    def shared_across(l):
+        wait(sh.at[l, pl.ds(0, 256), pl.ds(0, 256)], SH_R + l)
+
+        def step(to_e):
+            for from_zh in range(2):
+                part = shared_part(l, from_zh, own_columns)
+                put(part, part, SHX_S + l, SHX_R + l, (s, to_e, h))
+
+        peers(step)
+
+    def shared_forward(l):
+        across = sh.at[l, pl.ds(0, 256), pl.ds(0, 1920)]
+        wait(across, SHX_R + l)
+        for from_zh in range(2):
+            part = shared_part(l, from_zh, pl.ds(0, SHARED))
+            put(part, part, SHF_S + l, SHF_R + l, sibling)
+        wait(sh.at[l, pl.ds(0, 256)], SHF_R + l)
+        wait(sh.at[l, pl.ds(0, 256)], SHF_S + l)
+        wait(across, SHX_S + l)
+
+    shared_across(0)
     wait(rts.at[0], ROUTE_R)
     wait(rts.at[0], ROUTE_S)
     upper = one(iota((T, T), 0) < iota((T, T), 1)).astype(BF16)
@@ -210,14 +264,6 @@
         rows = nt(select, sh[l, :, 2048:2176])
         return rows[0:1], rows[1:2]
 
-    def shared_forward(l):
-        wait(sh.at[l, pl.ds(0, 256)], SH_R + l)
-        for from_zh in range(2):
-            part = sh.at[l, pl.ds(pl.multiple_of((2 * from_zh + c) * 128, 128), 128)]
-            put(part, part, SHF_S + l, SHF_R + l, sibling)
-        wait(sh.at[l, pl.ds(0, 256)], SHF_R + l)
-        wait(sh.at[l, pl.ds(0, 256)], SHF_S + l)
-
     def weights_forward(l):
         wait(w.at[l, pl.ds(0, 2)], W_R + l)
         for from_zh in range(2):
@@ -232,6 +278,8 @@
         rows_in = (x[...] if l == 0 else lo[0]).astype(F32)
         normed, _ = normalize(rows_in)
         shared_forward(l)
+        if l == 0:
+            shared_across(1)
         gain_one, gain_two = gains(l)
         first_in = (normed * gain_one).astype(BF16)
         qkv_s[l] = nn(first_in, sh[l, :, 0:1536]).astype(BF16)
@@ -263,6 +311,8 @@
         weights_forward(l)
         a2a_finish(2 * l, rows_b.at[l])
         weights_finish(l)
+        if l == 0:
+            weights_start(1, (1,))
         acc[...] = jnp.zeros_like(acc)
 
         def piece(j, carry):
@@ -282,34 +332,32 @@
             result = result + gat[l, :, k:k + 1] * mine
         lo[l] = result.astype(BF16)
 
-    def gw_a(l):
-        for to_zh in range(2):
-            put(gw.at[2 * to_zh + 1 - c], gwa.at[l, to_zh], GWA_S + l, GWA_R + l, sibling)
+    def gw_a(l, to_zh):
+        number = 2 * l + to_zh
+        put(gw.at[2 * to_zh + 1 - c], gwa.at[l, to_zh], GWA_S + number, GWA_R + number, sibling)
 
     def gw_b(l):
-        wait(gwa.at[l], GWA_R + l)
         for to_zh in range(2):
             j = 2 * to_zh + c
+            number = 2 * l + to_zh
             own = jnp.logical_and(s == l, zh == to_zh)
+            wait(gwa.at[l, to_zh], GWA_R + number)
             gw[j] = (gw[j].astype(F32) + gwa[l, to_zh].astype(F32)).astype(BF16)
-            send = GWB_S + 2 * l + to_zh
-            put_or_local(own, gw.at[j], ebuf.at[2 * s + zh], send, GWB_R, (l, e, j), send)
+            send = GWB_S + number
+            for from_zh, outs in enumerate(((eb_up0, eb_dn0), (eb_up1, eb_dn1))):
+                @pl.when(zh == from_zh)
+                def _():
+                    for u in range(2):
+                        put_or_local(own, gw.at[j, u], outs[u].at[s], send, GWB_R, (l, e, j), send)
 
     def gw_sent(l):
-        wait(gwa.at[l], GWA_S + l)
         for to_zh in range(2):
+            wait(gwa.at[l, to_zh], GWA_S + 2 * l + to_zh)
             wait(gw.at[0], GWB_S + 2 * l + to_zh)
 
     def gs_a(l):
         for to_zh in range(2):
             put(gs.at[l, 2 * to_zh + 1 - c], gsa.at[l, to_zh], GSA_S + l, GSA_R + l, sibling)
-
-    def peers(step):
-        def body(i, carry):
-            step(lax.rem(e + i, 16))
-            return carry
-
-        lax.fori_loop(1, 16, body, 0)
 
     def gs_b(l):
         wait(gsa.at[l], GSA_R + l)
@@ -387,19 +435,26 @@
         sbuf[...] = acc[...].astype(BF16).reshape(EXPERTS, SLOTS, D)
         a2a_start(5 + 2 * l, dr_b.at[l])
 
-        def weight_grads(j, carry):
+        def weight_grads(i, carry):
+            j = 2 * lax.rem(i, 2) + jnp.where(i < 2, 1 - c, c)
             gw[j, 1] = nn(act_t[j], g_b[l].reshape(EXPERTS * SLOTS, D)).astype(BF16)
             gw[j, 0] = nn(dp_t[j], rows_b[l].reshape(EXPERTS * SLOTS, D)).astype(BF16)
+            for to_zh in range(2):
+                @pl.when(i == to_zh)
+                def _():
+                    gw_a(l, to_zh)
             return carry
 
+        if l == 0:
+            gw_sent(1)
         lax.fori_loop(0, 4, weight_grads, 0)
-        gw_a(l)
         total = gate[0] * grad_gate[0] + gate[1] * grad_gate[1]
         chosen = choices(l)
         grad_logits = (
             chosen[0] * (gate[0] * (grad_gate[0] - total))
             + chosen[1] * (gate[1] * (grad_gate[1] - total))
         ).astype(BF16)
+        gw_b(l)
         hook_two()
         a2a_finish(5 + 2 * l, dr_b.at[l])
         gain_one, gain_two = gains(l)
@@ -463,39 +518,32 @@
         return None
 
     forward(0)
-    weights_start(1)
     forward(1)
     exchange(lo, lout, LO_S, LO_R)
     backward(1, cot[...].astype(F32), nothing, nothing)
 
     def first_hook():
-        gw_b(1)
         gs_b(1)
 
     def second_hook():
         gs_c(1)
 
-    def before_layer_zero():
-        first_hook()
-        gw_sent(1)
-
-    backward(0, li[1].astype(F32), before_layer_zero, second_hook)
+    backward(0, li[1].astype(F32), first_hook, second_hook)
     exchange(li, lig, LI_S, LI_R)
-    gw_b(0)
     gs_b(0)
     gs_c(0)
     gs_d()
     gw_sent(0)
     gs_sent(1)
     gs_sent(0)
-    wait(sh.at[0, pl.ds(0, 384)], SH_S)
+    wait(sh.at[0, pl.ds(0, 384), pl.ds(0, 256)], SH_S)
     wait(w.at[0, pl.ds(0, 3)], W_S)
     wait(gd.at[pl.ds(0, 15)], GSD_S)
     wait(gd, GSD_R)
     for out, send, recv in ((lout, LO_S, LO_R), (lig, LI_S, LI_R)):
         wait(out, recv)
         wait(out.at[0], send)
-    wait(ebuf.at[pl.ds(0, 3)], GWB_R)
+    wait(gw.at[pl.ds(0, 3)], GWB_R)
 
 
 def shards(
@@ -536,26 +584,27 @@
         pltpu.VMEM((2, T, D), BF16), pltpu.VMEM((2, T, D), BF16),
         pltpu.SemaphoreType.DMA((SEMS,)),
     ]
-    lout, lig, ebuf, gd = pl.pallas_call(
+    lout, lig, up0, up1, dn0, dn1, gd = pl.pallas_call(
         kernel,
         out_shape=(
             jax.ShapeDtypeStruct((2, T, D), BF16),
             jax.ShapeDtypeStruct((2, T, D), BF16),
-            jax.ShapeDtypeStruct((4, 2, 512, D), BF16),
+            jax.ShapeDtypeStruct((2, 512, D), BF16),
+            jax.ShapeDtypeStruct((2, 512, D), BF16),
+            jax.ShapeDtypeStruct((2, 512, D), BF16),
+            jax.ShapeDtypeStruct((2, 512, D), BF16),
             jax.ShapeDtypeStruct((16, 16, WIDE), BF16),
         ),
         in_specs=[vmem, vmem, vmem, anywhere, anywhere, anywhere],
-        out_specs=(anywhere,) * 4,
+        out_specs=(anywhere,) * 7,
         scratch_shapes=scratch,
         compiler_params=pltpu.CompilerParams(
-            has_side_effects=True, vmem_limit_bytes=63 * 1024 * 1024
+            has_side_effects=True, collective_id=0, vmem_limit_bytes=63 * 1024 * 1024
         ),
     )(x, cot, rt, shp, up_weight[0], down_weight[0])
     shape_out = (1, 2) + images.shape[1:]
     layer_out = lout[:, :ROWS].reshape(shape_out)
     layer_in_grad = lig[:, :ROWS].reshape(shape_out)
-    wide = ebuf.astype(F32)
-    sums = (wide[0::2] + wide[1::2])
     gathered = gd.reshape(256, WIDE)
     flat = jnp.concatenate([gathered[:128], gathered[128:]], axis=1).astype(F32)
     return (
@@ -566,8 +615,8 @@
         flat[:, 1536:2048][None],
         flat[:, 2081][None],
         flat[:, 2048:2080][None],
-        sums[:, 0][None],
-        sums[:, 1][None],
+        (up0.astype(F32) + up1.astype(F32))[None],
+        (dn0.astype(F32) + dn1.astype(F32))[None],
     )
 
 

time: 356 us -> 265 us (0.74)
  Pallas kernels: 333 us -> 246 us
    pallas_call x1, Pallas kernels: 333 us -> 246 us  [shards(): pl.pallas_call(kernel, out_shape=(jax.ShapeDtypeStruct((2, T, D), BF16),...]
where the time goes in v2:
time: 265 us
  Pallas kernels  246 us (93%)
  local copies, waits for them, and re-layouts  12.8 us (5%)
  other arithmetic  5.55 us (2%)
    pallas_call x1, Pallas kernels, shards(): pl.pallas_call(kernel, out_shape=(jax.ShapeDtypeStruct((2, T, D), BF16),...  246 us

profile of v2, /device:TPU:0, one launch (start us, length us, event | category | flops | bytes accessed | tf_op | source)
XLA Modules:
  0.0 265.2 jit_solution(10012573568754805239)
XLA Ops:
  0.6 0.0 copy-start.7
  0.7 0.0 copy-start.5
  0.7 0.8 convert_element_type.27
  1.4 0.1 convert_element_type.28
  1.5 0.6 pad.13.rt
  2.1 0.8 copy.44
  2.9 0.8 copy.45
  3.7 0.8 copy.43
  4.5 1.2 constant_dynamic-slice_fusion
  5.7 0.1 reshape.37
  5.8 0.7 pad.12.cot
  6.6 0.1 reshape.36
  6.6 0.7 pad.11.x
  7.4 0.0 copy-done.7
  7.4 0.0 copy-done.5
  7.4 1.0 concatenate.6.shp
  8.4 246.1 %shard_map.169 = (bf16[2,256,512]{2,1,0:T(8,128)(2,1)}, bf16[2,256,512]{2,1,0:T(8,128)(2,1)}, bf16[2,512,512]{2,1,0:T(8,128)(2,1)}, bf16[2,512,512]{2,1,0:T(8,12...) custom-call(bf16[256,512]{1,0:T(8,128)(2,1)} %pad.11.x, ...), custom_call_target="tpu_custom_call" | custom-call | tf_op jit(solution)/shard_map/pallas_call | solution.py:587
  254.4 0.0 copy-start.6
  254.4 1.1 slice.33
  255.5 0.0 copy-start.4
  255.5 0.3 copy.46
  255.9 0.9 copy.48
  256.8 0.0 copy-done.6
  256.8 0.3 copy.47
  257.1 0.9 copy.49
  258.0 0.0 copy-done.4
  258.1 0.7 convert_reduce_fusion
  258.8 0.7 copy.50
  259.5 0.0 copy-start.2
  259.5 0.0 copy-start.3
  259.5 0.7 convert_bitcast_fusion
  260.2 0.1 maximum_convert_fusion
  260.3 1.0 slice_bitcast_fusion
  261.3 0.0 copy-done.2
  261.3 0.0 copy-done.3
  261.3 0.0 copy-start
  261.3 0.0 copy-start.1
  261.3 1.6 add_bitcast_fusion.1
  262.9 0.0 copy-done
  262.9 0.6 copy-done.1
  263.5 1.6 add_bitcast_fusion
  (7 shorter events, 0.2 us)
Async XLA Ops:
  0.6 6.7 %copy-start.7 = (bf16[1,128,512]{2,1,0:T(8,128)(2,1)S(1)}, bf16[1,128,512]{2,1,0:T(8,128)(2,1)}, u32[]{:S(2)}) copy-start(bf16[1,128,512]{2,1,0:T(8,128)(2,1)} %param.14) | copy-start | bytes 393220
  0.7 6.7 %copy-start.5 = (bf16[1,128,1536]{2,1,0:T(8,128)(2,1)S(1)}, bf16[1,128,1536]{2,1,0:T(8,128)(2,1)}, u32[]{:S(2)}) copy-start(bf16[1,128,1536]{2,1,0:T(8,128)(2,1)} %param.13) | copy-start | bytes 1179652
  254.4 2.4 copy-start.6
  255.5 2.5 copy-start.4
  259.5 1.8 copy-start.2
  259.5 1.8 copy-start.3
  261.3 1.7 copy-start
  261.3 2.2 copy-start.1

commit v3 on v2

--- a/solution.py
+++ b/solution.py
@@ -196,7 +196,7 @@
                     put_or_local(own, dn.at[to_s], w.at[layer, h, 1], W_S, W_R + layer, device)
 
     weights_start(0, (0, 1))
-    weights_start(1, (0,))
+    weights_start(1, (0, 1))
 
     def peers(step):
         def body(i, carry):
@@ -311,8 +311,6 @@
         weights_forward(l)
         a2a_finish(2 * l, rows_b.at[l])
         weights_finish(l)
-        if l == 0:
-            weights_start(1, (1,))
         acc[...] = jnp.zeros_like(acc)
 
         def piece(j, carry):

time: 265 us -> 250 us (0.943)
  Pallas kernels: 246 us -> 230 us
    pallas_call x1, Pallas kernels: 246 us -> 230 us  [shards(): pl.pallas_call(kernel, out_shape=(jax.ShapeDtypeStruct((2, T, D), BF16),...]
where the time goes in v3:
time: 250 us; the launch traced here: 249 us
  Pallas kernels  230 us (92%)
  local copies, waits for them, and re-layouts  12.8 us (5%)
  other arithmetic  5.55 us (2%)
    pallas_call x1, Pallas kernels, shards(): pl.pallas_call(kernel, out_shape=(jax.ShapeDtypeStruct((2, T, D), BF16),...  230 us

profile of v3, /device:TPU:0, one launch (start us, length us, event | category | flops | bytes accessed | tf_op | source)
XLA Modules:
  0.0 249.0 jit_solution(6855263562174702120)
XLA Ops:
  0.6 0.0 copy-start.7
  0.7 0.0 copy-start.5
  0.7 0.8 convert_element_type.27
  1.4 0.1 convert_element_type.28
  1.5 0.6 pad.13.rt
  2.1 0.8 copy.44
  2.9 0.8 copy.45
  3.7 0.8 copy.43
  4.5 1.2 constant_dynamic-slice_fusion
  5.7 0.1 reshape.37
  5.8 0.7 pad.12.cot
  6.6 0.1 reshape.36
  6.6 0.7 pad.11.x
  7.4 0.0 copy-done.7
  7.4 0.0 copy-done.5
  7.4 1.0 concatenate.6.shp
  8.4 229.9 %shard_map.169 = (bf16[2,256,512]{2,1,0:T(8,128)(2,1)}, bf16[2,256,512]{2,1,0:T(8,128)(2,1)}, bf16[2,512,512]{2,1,0:T(8,128)(2,1)}, bf16[2,512,512]{2,1,0:T(8,12...) custom-call(bf16[256,512]{1,0:T(8,128)(2,1)} %pad.11.x, ...), custom_call_target="tpu_custom_call" | custom-call | tf_op jit(solution)/shard_map/pallas_call | solution.py:585
  238.3 0.0 copy-start.6
  238.3 1.1 slice.33
  239.4 0.0 copy-start.4
  239.4 0.3 copy.46
  239.7 0.9 copy.48
  240.6 0.0 copy-done.6
  240.7 0.3 copy.47
  241.0 0.9 copy.49
  241.9 0.0 copy-done.4
  242.0 0.7 convert_reduce_fusion
  242.7 0.7 copy.50
  243.4 0.0 copy-start.2
  243.4 0.0 copy-start.3
  243.4 0.7 convert_bitcast_fusion
  244.1 0.1 maximum_convert_fusion
  244.2 1.0 slice_bitcast_fusion
  245.1 0.0 copy-done.2
  245.1 0.0 copy-done.3
  245.1 0.0 copy-start
  245.1 0.0 copy-start.1
  245.1 1.6 add_bitcast_fusion.1
  246.8 0.0 copy-done
  246.8 0.6 copy-done.1
  247.4 1.6 add_bitcast_fusion
  (7 shorter events, 0.2 us)
Async XLA Ops:
  0.6 6.7 %copy-start.7 = (bf16[1,128,512]{2,1,0:T(8,128)(2,1)S(1)}, bf16[1,128,512]{2,1,0:T(8,128)(2,1)}, u32[]{:S(2)}) copy-start(bf16[1,128,512]{2,1,0:T(8,128)(2,1)} %param.14) | copy-start | bytes 393220
  0.7 6.7 %copy-start.5 = (bf16[1,128,1536]{2,1,0:T(8,128)(2,1)S(1)}, bf16[1,128,1536]{2,1,0:T(8,128)(2,1)}, u32[]{:S(2)}) copy-start(bf16[1,128,1536]{2,1,0:T(8,128)(2,1)} %param.13) | copy-start | bytes 1179652
  238.3 2.4 copy-start.6
  239.4 2.5 %copy-start.4 = (bf16[16,16,1152]{2,1,0:T(8,128)(2,1)S(1)}, bf16[16,16,1152]{2,1,0:T(8,128)(2,1)}, u32[]{:S(2)}) copy-start(bf16[16,16,1152]{2,1,0:T(8,128)(2,1)} %get-tuple-element.18) | copy-start | bytes 1769476
  243.4 1.8 copy-start.2
  243.4 1.8 copy-start.3
  245.1 1.7 copy-start
  245.1 2.2 copy-start.1

commit v4 on v3

--- a/solution.py
+++ b/solution.py
@@ -89,7 +89,7 @@
     qkv_s, o_s, hid, pick, gat,
     rows_b, ret_b, g_b, dr_b, sbuf, acc,
     act_t, gp_t, dp_t, dqkv,
-    gw, gwa, gs, gsa, gsb, gsc_s, gsc, gd_s, lo, li, sem,
+    gw, gwa, gs, gsa, gsb, gsc_s, gsc, gd_s, lo, li, mixed_s, first_s, narrow_s, sem,
 ):
     s, e, h = lax.axis_index("section"), lax.axis_index("expert"), lax.axis_index("shard")
     zh, c = lax.div(h, 2), lax.rem(h, 2)
@@ -400,6 +400,17 @@
         for to_zh in range(2):
             wait_unless(jnp.logical_and(s == l, zh == to_zh), gsc_s.at[l, to_zh], GSC_S + 2 * l + to_zh)
 
+    def shared_grads(l):
+        for j in range(4):
+            at = slice(j * 128, (j + 1) * 128)
+            part = tn(first_s[:, at], dqkv[...]).astype(BF16)
+            gs[l, j, 0:128, :] = part[:, 0:WIDE]
+            gs[l, j, 128:256, 0:384] = part[:, WIDE:1536]
+            gs[l, j, 128:256, 384:896] = tn(o_s[l, :, at], mixed_s[...]).astype(BF16)
+            gs[l, j, 128:256, 896:1024] = narrow_s[at]
+            gs[l, j, 128:256, 1024:1152] = jnp.zeros((128, 128), BF16)
+        gs_a(l)
+
     def backward(l, grad_out, hook_one, hook_two):
         gate = [gat[l, :, k:k + 1] for k in range(2)]
         grad_gate = [
@@ -453,8 +464,8 @@
             + chosen[1] * (gate[1] * (grad_gate[1] - total))
         ).astype(BF16)
         gw_b(l)
+        a2a_finish(5 + 2 * l, dr_b.at[l])
         hook_two()
-        a2a_finish(5 + 2 * l, dr_b.at[l])
         gain_one, gain_two = gains(l)
         returned = dr_b[l].reshape(EXPERTS * SLOTS, D)
         grad_second = nn(p_t[l, 0] + p_t[l, 1], returned) + nt(grad_logits, sh[l, :, 2048:2176])
@@ -465,10 +476,7 @@
         grad_mixed = grad_hidden.astype(BF16)
         router_grad = tn(second_in, grad_logits)
         grad_heads = nt(grad_mixed, sh[l, :, 1536:2048]).astype(BF16)
-        for j in range(4):
-            gs[l, j, 128:256, 384:896] = tn(
-                o_s[l, :, j * 128:(j + 1) * 128], grad_mixed
-            ).astype(BF16)
+        mixed_s[...] = grad_mixed
         for pair in range(4):
             at = pair * 128
             q = qkv_s[l, :, at:at + 128]
@@ -499,14 +507,8 @@
         li[l] = grad_in.astype(BF16)
         row8 = iota((8, D), 0)
         both = jnp.where(row8 == 0.0, gain_one_grad, jnp.where(row8 == 1.0, gain_two_grad, 0.0))
-        narrow = (router_grad + tn(both.astype(BF16), select)).astype(BF16)
-        for j in range(4):
-            part = tn(first_in[:, j * 128:(j + 1) * 128], dqkv[...]).astype(BF16)
-            gs[l, j, 0:128, :] = part[:, 0:WIDE]
-            gs[l, j, 128:256, 0:384] = part[:, WIDE:1536]
-            gs[l, j, 128:256, 896:1024] = narrow[j * 128:(j + 1) * 128]
-            gs[l, j, 128:256, 1024:1152] = jnp.zeros((128, 128), BF16)
-        gs_a(l)
+        narrow_s[...] = (router_grad + tn(both.astype(BF16), select)).astype(BF16)
+        first_s[...] = first_in
 
     def exchange(mine, out, send, recv):
         local(mine.at[s], out.at[s], recv)
@@ -521,13 +523,15 @@
     backward(1, cot[...].astype(F32), nothing, nothing)
 
     def first_hook():
+        shared_grads(1)
+
+    def second_hook():
         gs_b(1)
 
-    def second_hook():
-        gs_c(1)
-
     backward(0, li[1].astype(F32), first_hook, second_hook)
+    shared_grads(0)
     exchange(li, lig, LI_S, LI_R)
+    gs_c(1)
     gs_b(0)
     gs_c(0)
     gs_d()
@@ -580,6 +584,8 @@
         pltpu.VMEM((2, 2, 16, WIDE), BF16), pltpu.VMEM((4, 16, WIDE), BF16),
         pltpu.VMEM((16, WIDE), BF16),
         pltpu.VMEM((2, T, D), BF16), pltpu.VMEM((2, T, D), BF16),
+        pltpu.VMEM((T, D), BF16), pltpu.VMEM((T, D), BF16),
+        pltpu.VMEM((D, 128), BF16),
         pltpu.SemaphoreType.DMA((SEMS,)),
     ]
     lout, lig, up0, up1, dn0, dn1, gd = pl.pallas_call(

time: 250 us -> 255 us (1.020)
  Pallas kernels: 230 us -> 235 us
    pallas_call x1, Pallas kernels: 230 us -> 235 us  [shards(): pl.pallas_call(kernel, out_shape=(jax.ShapeDtypeStruct((2, T, D), BF16),...]
where the time goes in v4:
time: 255 us; the launch traced here: 254 us
  Pallas kernels  235 us (92%)
  local copies, waits for them, and re-layouts  12.8 us (5%)
  other arithmetic  5.55 us (2%)
    pallas_call x1, Pallas kernels, shards(): pl.pallas_call(kernel, out_shape=(jax.ShapeDtypeStruct((2, T, D), BF16),...  235 us

profile of v4, /device:TPU:0, one launch (start us, length us, event | category | flops | bytes accessed | tf_op | source)
XLA Modules:
  0.0 254.2 jit_solution(5737081305459436852)
XLA Ops:
  0.6 0.0 copy-start.7
  0.7 0.0 copy-start.5
  0.7 0.8 convert_element_type.27
  1.4 0.1 convert_element_type.28
  1.5 0.6 pad.13.rt
  2.1 0.8 copy.44
  2.9 0.8 copy.45
  3.7 0.8 copy.43
  4.5 1.2 constant_dynamic-slice_fusion
  5.7 0.1 reshape.37
  5.8 0.7 pad.12.cot
  6.6 0.1 reshape.36
  6.6 0.7 pad.11.x
  7.4 0.0 copy-done.7
  7.4 0.0 copy-done.5
  7.4 1.0 concatenate.6.shp
  8.4 235.1 %shard_map.169 = (bf16[2,256,512]{2,1,0:T(8,128)(2,1)}, bf16[2,256,512]{2,1,0:T(8,128)(2,1)}, bf16[2,512,512]{2,1,0:T(8,128)(2,1)}, bf16[2,512,512]{2,1,0:T(8,12...) custom-call(bf16[256,512]{1,0:T(8,128)(2,1)} %pad.11.x, ...), custom_call_target="tpu_custom_call" | custom-call | tf_op jit(solution)/shard_map/pallas_call | solution.py:591
  243.5 0.0 copy-start.6
  243.5 1.1 slice.33
  244.6 0.0 copy-start.4
  244.6 0.3 copy.46
  244.9 0.9 copy.48
  245.8 0.0 copy-done.6
  245.9 0.3 copy.47
  246.2 0.9 copy.49
  247.1 0.0 copy-done.4
  247.2 0.7 convert_reduce_fusion
  247.9 0.7 copy.50
  248.5 0.0 copy-start.2
  248.5 0.0 copy-start.3
  248.6 0.7 convert_bitcast_fusion
  249.3 0.1 maximum_convert_fusion
  249.4 1.0 slice_bitcast_fusion
  250.3 0.0 copy-done.2
  250.3 0.0 copy-done.3
  250.3 0.0 copy-start
  250.3 0.0 copy-start.1
  250.3 1.6 add_bitcast_fusion.1
  252.0 0.0 copy-done
  252.0 0.6 copy-done.1
  252.6 1.6 add_bitcast_fusion
  (7 shorter events, 0.2 us)
Async XLA Ops:
  0.6 6.7 %copy-start.7 = (bf16[1,128,512]{2,1,0:T(8,128)(2,1)S(1)}, bf16[1,128,512]{2,1,0:T(8,128)(2,1)}, u32[]{:S(2)}) copy-start(bf16[1,128,512]{2,1,0:T(8,128)(2,1)} %param.14) | copy-start | bytes 393220
  0.7 6.7 %copy-start.5 = (bf16[1,128,1536]{2,1,0:T(8,128)(2,1)S(1)}, bf16[1,128,1536]{2,1,0:T(8,128)(2,1)}, u32[]{:S(2)}) copy-start(bf16[1,128,1536]{2,1,0:T(8,128)(2,1)} %param.13) | copy-start | bytes 1179652
  243.5 2.4 copy-start.6
  244.6 2.5 copy-start.4
  248.5 1.8 copy-start.2
  248.5 1.8 copy-start.3
  250.3 1.7 copy-start
  250.3 2.2 copy-start.1
